TPU v7x, 32 devices: a whole 2x2x4 slice. The times are simulated.
32 devices in a mesh: dp: 8 (over z, y), blk: 2 (over core), tensor: 2 (over x).
Axes of the slice: x: 2, y: 2, z: 4, core: 2. Of those that a mesh axis runs over, the one named last changes fastest.
Arguments:
- block_in: bfloat16 [16, 512, 768], P('dp', 'blk'), may hold values from -6 to 6
- crop_shape: int32 [16], P('dp'), may hold values from 0 to 2, as said below
- norm_gains: float32 [2, 768], replicated, may hold values from 0.5 to 1.5
- shifts: float32 [4, 768], replicated, may hold values from -1.75 to 1.75
- qkv_weight: bfloat16 [3, 768, 768], P(None, None, 'tensor'), may hold values from -0.21875 to 0.21875
- qv_bias: float32 [2, 768], P(None, 'tensor'), may hold values from -1.75 to 1.75
- out_weight: bfloat16 [768, 768], P('tensor'), may hold values from -0.875 to 0.875
- up_weight: bfloat16 [768, 3072], P(None, 'tensor'), may hold values from -0.21875 to 0.21875
- up_bias: float32 [3072], P('tensor'), may hold values from -1.75 to 1.75
- down_weight: bfloat16 [3072, 768], P('tensor'), may hold values from -0.109375 to 0.109375
- tconv_weight: bfloat16 [768, 1024], replicated, may hold values from -0.21875 to 0.21875
- kernels: bfloat16 [2, 3456, 128], replicated, may hold values from -0.109375 to 0.109375
- grad_out: bfloat16 [16, 512, 768], P('dp', 'blk'), may hold values from -6 to 6
- grad_decoded: bfloat16 [16, 16, 16, 16, 128], P(('dp', 'tensor'), 'blk'), may hold values from -6 to 6
Outputs:
- block_out: bfloat16 [16, 512, 768], P('dp', 'blk')
- decoded: bfloat16 [16, 16, 16, 16, 128], P(('dp', 'tensor'), 'blk')
- grad_input: bfloat16 [16, 512, 768], P('dp', 'blk')
- grad_gains: float32 [2, 768], replicated
- grad_shifts: float32 [4, 768], replicated
- grad_qkv: float32 [3, 768, 768], P(None, None, 'tensor')
- grad_qv_bias: float32 [2, 768], P(None, 'tensor')
- grad_out_weight: float32 [768, 768], P('tensor')
- grad_up: float32 [768, 3072], P(None, 'tensor')
- grad_up_bias: float32 [3072], P('tensor')
- grad_down: float32 [3072, 768], P('tensor')
- grad_tconv: float32 [768, 1024], P(None, 'tensor')
- grad_kernels: float32 [2, 3456, 128], P(None, None, 'tensor')
Inputs may be any that keep to these rules, and one draw needn't show every extreme that they name: `crop_shape`: among the 2 items held by one index of dp, at least one has id 2.
All inputs are finite; a program needn't handle non-finite values.
Results may differ from a plain program's by a relative error of at most 0.025.
Values may be sent and summed in bfloat16 or wider, within the bound.
A program may use at most 256 MiB of HBM per device.

v0:
```python
import jax
import jax.numpy as jnp
from jax import lax
from jax.sharding import PartitionSpec as P

GRID = 8
HD = 64


def extended(block, sides, width):
    for axis, dim in sides:
        count = lax.axis_size(axis)
        forward = [(i, i + 1) for i in range(count - 1)]
        backward = [(target, source) for source, target in forward]
        low = lax.ppermute(
            lax.slice_in_dim(block, block.shape[dim] - width, None, axis=dim), axis, forward
        )
        high = lax.ppermute(lax.slice_in_dim(block, 0, width, axis=dim), axis, backward)
        block = jnp.concatenate([low, block, high], axis=dim)
    return block


def layer_norm(value, gain, shift):
    centre = value - jnp.mean(value, axis=-1, keepdims=True)
    spread = jnp.mean(centre * centre, axis=-1, keepdims=True)
    return centre * lax.rsqrt(spread + 1e-06) * gain + shift


def patch_valid(crop_ids):
    extent_depth = jnp.where(
        crop_ids == 0, GRID * 3 // 4, jnp.where(crop_ids == 1, GRID // 2, GRID)
    )
    extent_side = jnp.where(crop_ids == 0, GRID * 3 // 4, GRID)
    places = jnp.arange(GRID * GRID * GRID, dtype=jnp.int32)
    depth = places // (GRID * GRID)
    across = places // GRID % GRID
    along = places % GRID
    inside = (
        (depth[None, :] < extent_depth[:, None])
        & (across[None, :] < extent_side[:, None])
        & (along[None, :] < extent_side[:, None])
    )
    return inside.astype(jnp.float32)


def voxel_mask(valid):
    grid = valid.reshape(valid.shape[0], -1, GRID, GRID)
    for axis_at in (1, 2, 3):
        grid = jnp.repeat(grid, 2, axis=axis_at)
    return grid[..., None]


def to_voxels(lifted):
    count, rows, columns = lifted.shape
    depth = rows // (GRID * GRID)
    channels = columns // 8
    shaped = lifted.reshape(count, depth, GRID, GRID, 2, 2, 2, channels)
    return shaped.transpose(0, 1, 4, 2, 5, 3, 6, 7).reshape(
        count, 2 * depth, 2 * GRID, 2 * GRID, channels
    )


def from_voxels(field):
    count, depth, height, breadth, channels = field.shape
    shaped = field.reshape(count, depth // 2, 2, GRID, 2, GRID, 2, channels)
    return shaped.transpose(0, 1, 3, 5, 2, 4, 6, 7).reshape(
        count, depth // 2 * GRID * GRID, 8 * channels
    )


def columns_of(padded):
    count, depth, height, breadth, channels = padded.shape
    depth, height, breadth = (depth - 2, height - 2, breadth - 2)
    pieces = [
        padded[
            :, deep_at : deep_at + depth, high_at : high_at + height, wide_at : wide_at + breadth, :
        ]
        for deep_at in range(3)
        for high_at in range(3)
        for wide_at in range(3)
    ]
    return jnp.concatenate(pieces, axis=-1).reshape(count * depth * height * breadth, 27 * channels)


def with_rims(field):
    deeper = extended(field, (("blk", 1),), 1)
    return jnp.pad(deeper, ((0, 0), (0, 0), (1, 1), (1, 1), (0, 0)))


def channel_sums(first_term, second_term):
    return lax.psum(
        (jnp.sum(first_term, axis=(1, 2, 3)), jnp.sum(second_term, axis=(1, 2, 3))), "blk"
    )


def norm_forward(level, voxel_valid, voxel_count):
    sums = channel_sums(voxel_valid * level, voxel_valid * level * level)
    mean = (sums[0] / voxel_count)[:, None, None, None, :]
    second = (sums[1] / voxel_count)[:, None, None, None, :]
    scale = lax.rsqrt(second - mean * mean + 1e-05)
    return ((level - mean) * scale, scale)


def norm_backward(dnormed, normed, scale, voxel_valid, voxel_count):
    sums = channel_sums(dnormed, dnormed * normed)
    mean_grad = (sums[0] / voxel_count)[:, None, None, None, :]
    mean_cross = (sums[1] / voxel_count)[:, None, None, None, :]
    return scale * (dnormed - voxel_valid * (mean_grad + normed * mean_cross))


def conv_forward(field, kernel):
    padded = with_rims(field)
    level = jnp.dot(columns_of(padded), kernel, preferred_element_type=jnp.float32)
    return (padded, level.reshape(field.shape[:4] + (kernel.shape[1],)))


def conv_input_grad(dlevel, kernel):
    channels = kernel.shape[1]
    flipped = (
        kernel.reshape(27, channels, channels)[::-1]
        .transpose(0, 2, 1)
        .reshape(27 * channels, channels)
    )
    result = jnp.dot(columns_of(with_rims(dlevel)), flipped, preferred_element_type=jnp.float32)
    return result.reshape(dlevel.shape[:4] + (channels,))


def body(
    block_in,
    crop_shape,
    norm_gains,
    shifts,
    qkv_weight,
    qv_bias,
    out_weight,
    up_weight,
    up_bias,
    down_weight,
    tconv_weight,
    kernels,
    grad_out,
    grad_decoded,
):
    item_count, slab_rows, width_all = block_in.shape
    local_width = qkv_weight.shape[2]
    local_heads = local_width // HD
    scale_factor = HD ** (-0.5)
    valid_full = patch_valid(crop_shape)
    patch_total = valid_full.shape[1]
    valid_local = lax.dynamic_slice_in_dim(
        valid_full, lax.axis_index("blk") * slab_rows, slab_rows, 1
    )
    key_valid = valid_full[:, None, None, :] > 0.5
    inputs = block_in.astype(jnp.float32)
    normed_one = layer_norm(inputs, norm_gains[0], shifts[0]).astype(jnp.bfloat16)
    project = jnp.einsum(
        "isd,cde->cise", normed_one, qkv_weight, preferred_element_type=jnp.float32
    )
    query = (project[0] + qv_bias[0]).astype(jnp.bfloat16)
    keys = project[1].astype(jnp.bfloat16)
    values = (project[2] + qv_bias[1]).astype(jnp.bfloat16)
    key_value = lax.all_gather(jnp.stack([keys, values]), "blk", axis=2, tiled=True)
    query_heads = query.reshape(item_count, slab_rows, local_heads, HD)
    key_heads = key_value[0].reshape(item_count, patch_total, local_heads, HD)
    value_heads = key_value[1].reshape(item_count, patch_total, local_heads, HD)

    def score_block():
        raw = (
            jnp.einsum(
                "iqhe,ikhe->ihqk", query_heads, key_heads, preferred_element_type=jnp.float32
            )
            * scale_factor
        )
        return jnp.where(key_valid, raw, -1000000000.0)

    scores = score_block()
    top_score = jnp.max(scores, axis=-1, keepdims=True)
    weights = jnp.exp(scores - top_score)
    weight_sum = jnp.sum(weights, axis=-1, keepdims=True)
    probs = weights / weight_sum
    log_total = top_score + jnp.log(weight_sum)
    mixed = jnp.einsum(
        "ihqk,ikhe->iqhe",
        probs.astype(jnp.bfloat16),
        value_heads,
        preferred_element_type=jnp.float32,
    )
    mixed_low = mixed.reshape(item_count, slab_rows, local_width).astype(jnp.bfloat16)
    partial_value = jnp.einsum(
        "ise,ed->isd", mixed_low, out_weight, preferred_element_type=jnp.float32
    )
    partial_value = lax.optimization_barrier(partial_value.astype(jnp.bfloat16)).astype(jnp.float32)
    middle = inputs + (
        lax.psum(partial_value.astype(jnp.bfloat16), "tensor").astype(jnp.float32) + shifts[2]
    )
    normed_two = layer_norm(middle, norm_gains[1], shifts[1]).astype(jnp.bfloat16)
    hidden = (
        jnp.einsum("isd,df->isf", normed_two, up_weight, preferred_element_type=jnp.float32)
        + up_bias
    )
    active_low = jax.nn.gelu(hidden).astype(jnp.bfloat16)
    partial_value = jnp.einsum(
        "isf,fd->isd", active_low, down_weight, preferred_element_type=jnp.float32
    )
    partial_value = lax.optimization_barrier(partial_value.astype(jnp.bfloat16)).astype(jnp.float32)
    block_out = middle + (
        lax.psum(partial_value.astype(jnp.bfloat16), "tensor").astype(jnp.float32) + shifts[3]
    )
    out_low = block_out.astype(jnp.bfloat16)
    per_device = item_count // lax.axis_size("tensor")
    first_item = lax.axis_index("tensor") * per_device
    tapped = lax.dynamic_slice_in_dim(out_low, first_item, per_device, 0)
    my_valid = lax.dynamic_slice_in_dim(valid_local, first_item, per_device, 0)
    voxel_count = 8.0 * jnp.sum(
        lax.dynamic_slice_in_dim(valid_full, first_item, per_device, 0), axis=1, keepdims=True
    )
    voxel_valid = voxel_mask(my_valid)
    lifted = jnp.einsum("isd,dk->isk", tapped, tconv_weight, preferred_element_type=jnp.float32)
    field_one = (to_voxels(lifted) * voxel_valid).astype(jnp.bfloat16)
    padded_one, level = conv_forward(field_one, kernels[0])
    normed_dec_one, scale_one = norm_forward(level, voxel_valid, voxel_count)
    field_two = (jax.nn.silu(normed_dec_one) * voxel_valid).astype(jnp.bfloat16)
    padded_two, level = conv_forward(field_two, kernels[1])
    normed_dec_two, scale_two = norm_forward(level, voxel_valid, voxel_count)
    decoded = (jax.nn.silu(normed_dec_two) * voxel_valid).astype(jnp.bfloat16)
    channels = kernels.shape[2]
    silu_two, silu_back_two = jax.vjp(jax.nn.silu, normed_dec_two)
    dnormed = silu_back_two(grad_decoded.astype(jnp.float32) * voxel_valid)[0]
    dlevel = norm_backward(dnormed, normed_dec_two, scale_two, voxel_valid, voxel_count).astype(
        jnp.bfloat16
    )
    grad_kernel_two = jnp.einsum(
        "rk,rc->kc",
        columns_of(padded_two),
        dlevel.reshape(-1, channels),
        preferred_element_type=jnp.float32,
    )
    dfield_two = conv_input_grad(dlevel, kernels[1])
    silu_one, silu_back_one = jax.vjp(jax.nn.silu, normed_dec_one)
    dnormed = silu_back_one(dfield_two * voxel_valid)[0]
    dlevel = norm_backward(dnormed, normed_dec_one, scale_one, voxel_valid, voxel_count).astype(
        jnp.bfloat16
    )
    grad_kernel_one = jnp.einsum(
        "rk,rc->kc",
        columns_of(padded_one),
        dlevel.reshape(-1, channels),
        preferred_element_type=jnp.float32,
    )
    dfield_one = conv_input_grad(dlevel, kernels[0])
    dlifted = from_voxels(dfield_one * voxel_valid).astype(jnp.bfloat16)
    grad_tconv = jnp.einsum("isd,isk->dk", tapped, dlifted, preferred_element_type=jnp.float32)
    dtapped = jnp.einsum("isk,dk->isd", dlifted, tconv_weight, preferred_element_type=jnp.float32)
    grad_kernel_pair = jnp.stack([grad_kernel_one, grad_kernel_two])
    dec_parts = (
        lax.psum_scatter(
            grad_tconv.astype(jnp.bfloat16), "tensor", scatter_dimension=1, tiled=True
        ).astype(jnp.float32),
        lax.psum_scatter(
            grad_kernel_pair.astype(jnp.bfloat16), "tensor", scatter_dimension=2, tiled=True
        ).astype(jnp.float32),
    )
    dtap_all = lax.all_gather(dtapped.astype(jnp.bfloat16), "tensor", axis=0, tiled=True).astype(
        dtapped.dtype
    )
    dout = grad_out.astype(jnp.float32) + dtap_all
    ddown = dout.astype(jnp.bfloat16)
    grad_shift_three = jnp.sum(ddown.astype(jnp.float32), axis=(0, 1))
    grad_down = jnp.einsum("isf,isd->fd", active_low, ddown, preferred_element_type=jnp.float32)
    dactive = jnp.einsum("isd,fd->isf", ddown, down_weight, preferred_element_type=jnp.float32)
    gelu_value, gelu_back = jax.vjp(jax.nn.gelu, hidden)
    dhidden = gelu_back(dactive)[0].astype(jnp.bfloat16)
    grad_up_bias = jnp.sum(dhidden.astype(jnp.float32), axis=(0, 1))
    grad_up = jnp.einsum("isd,isf->df", normed_two, dhidden, preferred_element_type=jnp.float32)
    dnormed_two = lax.psum(
        jnp.einsum("isf,df->isd", dhidden, up_weight, preferred_element_type=jnp.float32).astype(
            jnp.bfloat16
        ),
        "tensor",
    ).astype(jnp.float32)
    norm_value, norm_back_two = jax.vjp(layer_norm, middle, norm_gains[1], shifts[1])
    dmid_norm, grad_gain_one, grad_shift_one = norm_back_two(dnormed_two)
    dmiddle = dout + dmid_norm
    dattn = dmiddle.astype(jnp.bfloat16)
    grad_shift_two = jnp.sum(dattn.astype(jnp.float32), axis=(0, 1))
    grad_out_weight = jnp.einsum(
        "ise,isd->ed", mixed_low, dattn, preferred_element_type=jnp.float32
    )
    dmixed = jnp.einsum(
        "isd,ed->ise", dattn, out_weight, preferred_element_type=jnp.float32
    ).astype(jnp.bfloat16)
    dmixed_heads = dmixed.reshape(item_count, slab_rows, local_heads, HD)
    probs_again = jnp.exp(score_block() - log_total)
    dprobs = jnp.einsum(
        "iqhe,ikhe->ihqk", dmixed_heads, value_heads, preferred_element_type=jnp.float32
    )
    dprobs = lax.optimization_barrier(dprobs.astype(jnp.bfloat16)).astype(jnp.float32)
    dscores = (
        probs_again * (dprobs - jnp.sum(probs_again * dprobs, axis=-1, keepdims=True))
    ).astype(jnp.bfloat16)
    dquery = (
        jnp.einsum("ihqk,ikhe->iqhe", dscores, key_heads, preferred_element_type=jnp.float32)
        * scale_factor
    ).astype(jnp.bfloat16)
    dkey_part = (
        jnp.einsum("ihqk,iqhe->ikhe", dscores, query_heads, preferred_element_type=jnp.float32)
        * scale_factor
    )
    dvalue_part = jnp.einsum(
        "ihqk,iqhe->ikhe",
        probs_again.astype(jnp.bfloat16),
        dmixed_heads,
        preferred_element_type=jnp.float32,
    )
    kv_parts = jnp.stack(
        [
            dkey_part.reshape(item_count, patch_total, local_width),
            dvalue_part.reshape(item_count, patch_total, local_width),
        ]
    )
    kv_grads = lax.psum_scatter(
        kv_parts.astype(jnp.bfloat16), "blk", scatter_dimension=2, tiled=True
    )
    dproject = jnp.stack(
        [dquery.reshape(item_count, slab_rows, local_width), kv_grads[0], kv_grads[1]]
    )
    grad_qv_bias = jnp.stack(
        [
            jnp.sum(dproject[0].astype(jnp.float32), axis=(0, 1)),
            jnp.sum(dproject[2].astype(jnp.float32), axis=(0, 1)),
        ]
    )
    grad_qkv = jnp.einsum("isd,cise->cde", normed_one, dproject, preferred_element_type=jnp.float32)
    dnormed_one = lax.psum(
        jnp.einsum(
            "cise,cde->isd", dproject, qkv_weight, preferred_element_type=jnp.float32
        ).astype(jnp.bfloat16),
        "tensor",
    ).astype(jnp.float32)
    norm_first, norm_back_one = jax.vjp(layer_norm, inputs, norm_gains[0], shifts[0])
    din_norm, grad_gain_zero, grad_shift_zero = norm_back_one(dnormed_one)
    grad_input = (dmiddle + din_norm).astype(jnp.bfloat16)
    grad_gains = jnp.stack([grad_gain_zero, grad_gain_one])
    grad_shifts = jnp.stack([grad_shift_zero, grad_shift_one, grad_shift_two, grad_shift_three])
    summed_all = lax.psum(
        (
            grad_gains,
            grad_shifts,
            grad_qkv,
            grad_qv_bias,
            grad_out_weight,
            grad_up,
            grad_up_bias,
            grad_down,
            dec_parts[0],
            dec_parts[1],
        ),
        ("dp", "blk"),
    )
    summed = summed_all[:8]
    dec_final = summed_all[8:]
    return (
        out_low,
        decoded,
        grad_input,
        summed[0],
        summed[1],
        summed[2],
        summed[3],
        summed[4],
        summed[5],
        summed[6],
        summed[7],
        dec_final[0],
        dec_final[1],
    )


def solution(mesh):
    return jax.shard_map(
        body,
        mesh=mesh,
        in_specs=(
            P("dp", "blk", None),
            P("dp"),
            P(),
            P(),
            P(None, None, "tensor"),
            P(None, "tensor"),
            P("tensor", None),
            P(None, "tensor"),
            P("tensor"),
            P("tensor", None),
            P(),
            P(),
            P("dp", "blk", None),
            P(("dp", "tensor"), "blk", None, None, None),
        ),
        out_specs=(
            P("dp", "blk", None),
            P(("dp", "tensor"), "blk", None, None, None),
            P("dp", "blk", None),
            P(),
            P(),
            P(None, None, "tensor"),
            P(None, "tensor"),
            P("tensor", None),
            P(None, "tensor"),
            P("tensor"),
            P("tensor", None),
            P(None, "tensor"),
            P(None, None, "tensor"),
        ),
        check_vma=False,
    )
```

profile of v0, /device:TPU:0, one launch (start us, length us, event | category | flops | bytes accessed | tf_op | source)
XLA Modules:
  0.0 810.0 jit_solution(615800238587380878)
XLA Ops:
  12.5 3.1 fusion.63
  18.2 11.3 %all-gather.3.cloned.1.call-done = bf16[2,2,512,384]{3,2,0,1:T(8,128)(2,1)} async-done(((bf16[2,2,256,384]{3,2,0,1:T(8,128)(2,1)}), bf16[2,2,512,384]{3,2,0,1:T(8,128)(2,1)}) %all-gather.3.cloned.1.call-update) | async-done | bytes 1572880 | tf_op jit(solution)/shard_map/all_gather | solution.py:162
  29.5 2.4 fusion.160
  34.5 2.8 fusion.165
  39.0 2.2 fusion.95
  43.5 35.6 %all-reduce.19.cloned.1.call-done = bf16[2,256,768]{2,1,0:T(8,128)(2,1)} async-done(((bf16[2,256,768]{2,1,0:T(8,128)(2,1)}), bf16[2,256,768]{2,1,0:T(8,128)(2,1)}) %all-reduce.19.cloned.1.call-update) | async-done | bytes 786448 | tf_op jit(solution)/shard_map/psum | solution.py:194
  82.2 3.4 convolution_add_fusion
  87.3 2.8 fusion.79
  90.6 2.6 copy.129
  93.4 31.3 %all-reduce.21.cloned.1.call-done = bf16[2,256,768]{2,1,0:T(8,128)(2,1)} async-done(((bf16[2,256,768]{2,1,0:T(8,128)(2,1)}), bf16[2,256,768]{2,1,0:T(8,128)(2,1)}) %all-reduce.21.cloned.1.call-update) | async-done | bytes 786448 | tf_op jit(solution)/shard_map/psum | solution.py:207
  127.5 2.0 convolution_bitcast_fusion.4
  134.2 3.0 collective-permute-start
  151.1 5.0 copy-done.59
  156.3 3.3 constant_dynamic-update-slice_fusion.54
  163.6 4.9 fusion.106
  168.6 2.4 all-reduce.10
  173.9 3.4 collective-permute-start.2
  177.4 2.2 reverse_bitcast_fusion
  187.5 5.1 copy-done.60
  192.7 3.3 constant_dynamic-update-slice_fusion.81
  200.0 4.9 fusion.107
  204.9 2.4 all-reduce.9
  207.4 3.2 fusion.156
  210.6 2.4 all-reduce.8
  213.1 1.9 multiply_convert_fusion.3
  217.1 3.0 collective-permute-start.4
  220.1 2.2 reverse_bitcast_fusion.1
  222.3 2.4 copy.105
  224.7 2.2 copy.103
  234.7 5.4 fusion.155
  240.1 2.4 all-reduce.7
  242.5 1.9 fusion.188
  245.7 3.4 collective-permute-start.6
  256.7 4.0 fusion.91
  262.3 12.2 %all-gather = bf16[512,768]{1,0:T(8,128)(2,1)S(1)} all-gather(bf16[256,768]{1,0:T(8,128)(2,1)S(1)} %convolution_convert_fusion.4), channel_id=2, replica_groups=mesh['dp'=8,'blk'=2,'tensor'=2] {'tensor'}, dimensions={0}, use_global_device_ids=true | all-gather | bytes 1179648 | tf_op jit(solution)/shard_map/all_gather | solution.py:263
  274.5 3.7 convert_reduce_fusion
  279.4 2.3 fusion.76
  281.9 8.2 %fusion.28 = bf16[1,3456,128]{2,1,0:T(8,128)(2,1)} fusion(bf16[1,8,16,16,3456]{4,3,2,1,0:T(8,128)(2,1)} %get-tuple-element.159, bf16[1,8,16,16,128]{4,3,2,1,0:T(8,128)(2,1)S(1)} %copy-done.17), kind=kOutput, calls=%fused_computation.24 | convolution fusion | flops 1812381696 | bytes 15564800 | tf_op jit(solution)/shard_map/rk,rc->kc/dot_general | solution.py:232
  290.0 26.2 %all-reduce.23.cloned.1.call-done = bf16[2,256,768]{2,1,0:T(8,128)(2,1)} async-done(((bf16[2,256,768]{2,1,0:T(8,128)(2,1)}), bf16[2,256,768]{2,1,0:T(8,128)(2,1)}) %all-reduce.23.cloned.1.call-update) | async-done | bytes 786448 | tf_op jit(solution)/shard_map/psum | solution.py:275
  316.3 2.6 convert_reduce_fusion.2
  318.8 2.8 fusion.71
  324.6 1.9 copy.107
  326.5 3.9 convolution_convert_fusion
  330.5 5.0 fusion.82
  335.4 2.3 copy.109
  337.7 4.9 fusion.8
  342.7 3.7 fusion.10
  349.6 2.3 copy.108
  351.9 2.7 pad_maximum_fusion.1
  354.9 9.6 %fusion.25 = bf16[1,3456,128]{2,1,0:T(8,128)(2,1)S(1)} fusion(bf16[1,8,16,16,3456]{4,3,2,1,0:T(8,128)(2,1)} %get-tuple-element.133, f32[8,16,16,128]{3,2,1,0:T(8,128)} %get-tuple-element.200, f32[128]{0:T(128)S(1)} %divide_bitcast_fusion, f32[128]{0:T(128)S(1)} %divide_bitcast_fusion.1, f32[128]{0:T(128)S(1)} %get-tuple-element.123, ...), kind=kOutput, calls=%fused_computation.23 | convolution fusion | flops 1814478848 | bytes 17147904 | tf_op jit(solution)/shard_map/rk,rc->kc/dot_general | solution.py:244
  365.8 5.6 copy.114
  371.4 3.6 convert_reduce_fusion.7
  375.3 3.9 bitcast_convert_fusion
  382.6 5.4 convolution_bitcast_fusion.1
  388.1 4.3 convolution_bitcast_fusion
  393.9 3.1 convolution_bitcast_fusion.2
  397.0 55.4 %all-reduce.27.cloned.1.call-done = (bf16[2,256,768]{2,1,0:T(8,128)(2,1)}, bf16[2,3456,128]{1,0,2:T(2,128)(2,1)}) async-done(((bf16[2,256,768]{2,1,0:T(8,128)(2,1)}, bf16[2,3456,128]{1,0,2:T(2,128)(2,1)}), (bf16[2,256,768]{2,1,0:T(8,128)(2,1)}, bf16[2,3456,128]{1,0,2:T(2,128)(2,1)})) %all-reduce.27.cloned.1.call-update) | async-done | bytes 2555920 | tf_op jit(solution)/shard_map/psum | solution.py:334
  452.4 3.0 dynamic-slice_convert_fusion
  456.3 24.6 %reduce-scatter.5.cloned.1.call-done = bf16[768,512]{1,0:T(8,128)(2,1)} async-done(((bf16[768,1024]{1,0:T(8,128)(2,1)}), bf16[768,512]{1,0:T(8,128)(2,1)}) %reduce-scatter.5.cloned.1.call-update) | async-done | bytes 786448 | tf_op jit(solution)/shard_map/reduce_scatter | solution.py:256
  483.6 97.2 %all-reduce.28 = (f32[2,768]{1,0:T(2,128)}, f32[4,768]{1,0:T(4,128)}, f32[2,384]{1,0:T(2,128)}, f32[1536]{0:T(1024)}, f32[768,512]{1,0:T(8,128)}) all-reduce(f32[2,768]{1,0:T(2,128)S(1)} %pad_maximum_fusion.15, f32[4,768]{1,0:T(4,128)S(1)} %pad_maximum_fusion.14, ...), channel_id=1, replica_groups=mesh['dp'=8,'blk'=2,'tensor'=2] {'dp','blk'}, use_global_device_ids=true, to_apply=%region_35.36 | all-reduce | flops 400128 | bytes 2414592 | tf_op jit(solution)/shard_map/psum | solution.py:345
  582.3 206.9 %all-reduce.25.cloned.1.call-done = (f32[3,768,384]{1,2,0:T(8,128)}, f32[384,768]{1,0:T(8,128)}, f32[768,1536]{1,0:T(8,128)}, f32[1536,768]{1,0:T(8,128)}, f32[2,3456,64]{1,0,2:T(2,128)}) async-done(((f32[3,768,384]{1,2,0:T(8,128)}, f32[384,768]{1,0:T(8,128)}, f32[768,1536]{1,0:T(8,128)}, f32[1536,768]{1,0:T(8,128)}, f32[2,3456,64]{1,0,2:T(2,128)}), (f32[3,768,384]{1,2,0:T(8,128)}, f32[384,768]{1,0:T(8,128)}, ...) | async-done | bytes 15925264 | tf_op jit(solution)/shard_map/psum | solution.py:345
  789.3 5.3 copy.115
  798.0 2.4 copy.305
  800.5 2.2 copy.306
  (451 shorter events, 100.7 us)
Async XLA Ops:
  7.2 80.2 %copy-start = (bf16[1536,768]{1,0:T(8,128)(2,1)S(1)}, bf16[1536,768]{1,0:T(8,128)(2,1)}, u32[]{:S(2)}) copy-start(bf16[1536,768]{1,0:T(8,128)(2,1)} %param.23) | copy-start | bytes 7077892
  7.2 22.3 %all-gather.3.cloned.1.call-start = ((), (), s32[]{:S(2)}) async-start(), calls=%async_computation.2 | async-start | bytes 2359296 | tf_op jit(solution)/shard_map/all_gather | solution.py:162
  8.7 7.0 copy-start.57
  10.8 4.9 copy-start.61
  12.5 69.6 %copy-start.77 = (f32[768]{0:T(1024)}, f32[768]{0:T(1024)S(1)}, u32[]{:S(2)}) copy-start(f32[768]{0:T(1024)S(1)} %get-tuple-element.84) | copy-start | bytes 9220
  16.8 62.3 %all-reduce.19.cloned.1.call-start = ((), (), s32[]{:S(2)}) async-start(), calls=%async_computation.3 | async-start | bytes 1572864 | tf_op jit(solution)/shard_map/psum | solution.py:194
  18.1 19.2 %copy-start.53 = (f32[6,64]{1,0:T(8,128)}, f32[6,64]{1,0:T(8,128)S(1)}, u32[]{:S(2)}) copy-start(f32[6,64]{1,0:T(8,128)S(1)} %add.313) | copy-start | bytes 4612
  34.5 4.3 copy-start.20
  39.0 40.1 %copy-start.3 = (bf16[2,256,768]{2,1,0:T(8,128)(2,1)S(1)}, bf16[2,256,768]{2,1,0:T(8,128)(2,1)}, u32[]{:S(2)}) copy-start(bf16[2,256,768]{2,1,0:T(8,128)(2,1)} %param.14) | copy-start | bytes 2359300
  41.2 41.0 %copy-start.79 = (f32[1536]{0:T(1024)S(1)}, f32[1536]{0:T(1024)}, u32[]{:S(2)}) copy-start(f32[1536]{0:T(1024)} %param.22) | copy-start | bytes 18436
  43.5 81.3 %all-reduce.21.cloned.1.call-start = ((), (), s32[]{:S(2)}) async-start(), calls=%async_computation.4 | async-start | bytes 1572864 | tf_op jit(solution)/shard_map/psum | solution.py:207
  90.2 226.0 %all-reduce.23.cloned.1.call-start = ((), (), s32[]{:S(2)}) async-start(), calls=%async_computation.5 | async-start | bytes 1572864 | tf_op jit(solution)/shard_map/psum | solution.py:275
  129.5 7.7 copy-start.35
  132.9 9.2 %collective-permute-start.1 = (bf16[1,1,16,16,128]{4,3,2,1,0:T(8,128)(2,1)}, bf16[1,1,16,16,128]{4,3,2,1,0:T(8,128)(2,1)S(1)}, u32[]{:S(2)}, u32[]{:S(2)}) collective-permute-start(bf16[1,1,16,16,128]{4,3,2,1,0:T(8,128)(2,1)} %get-tuple-element.193), channel_id=1, source_target_pairs={{2,0},{3,1},{6,4},{7,5},{10,8},{11,9},{14,12},{15,13},{18,16},{19,... | collective-permute-start | bytes 196616 | tf_op jit(solution)/shard_map/ppermute | solution.py:18
  134.2 8.0 collective-permute-start
  151.1 5.0 copy-start.59
  172.6 6.9 collective-permute-start.3
  173.9 5.6 collective-permute-start.2
  187.4 5.1 copy-start.60
  215.8 11.1 %collective-permute-start.5 = (bf16[1,1,16,16,128]{4,3,2,1,0:T(8,128)(2,1)S(1)}, bf16[1,1,16,16,128]{4,3,2,1,0:T(8,128)(2,1)S(1)}, u32[]{:S(2)}, u32[]{:S(2)}) collective-permute-start(bf16[1,1,16,16,128]{4,3,2,1,0:T(8,128)(2,1)S(1)} %get-tuple-element.189), channel_id=1, source_target_pairs={{2,0},{3,1},{6,4},{7,5},{10,8},{11,9},{14,12},{15,13},{18,16},{19,... | collective-permute-start | bytes 196616 | tf_op jit(solution)/shard_map/ppermute | solution.py:18
  217.1 9.8 %collective-permute-start.4 = (bf16[1,1,16,16,128]{4,3,2,1,0:T(8,128)(2,1)S(1)}, bf16[1,1,16,16,128]{4,3,2,1,0:T(8,128)(2,1)S(1)}, u32[]{:S(2)}, u32[]{:S(2)}) collective-permute-start(bf16[1,1,16,16,128]{4,3,2,1,0:T(8,128)(2,1)S(1)} %get-tuple-element.188), channel_id=1, source_target_pairs={{0,2},{1,3},{4,6},{5,7},{8,10},{9,11},{12,14},{13,15},{16,18},{17,... | collective-permute-start | bytes 196616 | tf_op jit(solution)/shard_map/ppermute | solution.py:15
  244.4 4.8 collective-permute-start.7
  245.7 3.9 collective-permute-start.6
  256.7 5.0 copy-start.42
  260.7 13.8 %copy-start.49 = (bf16[2,256,768]{2,1,0:T(8,128)(2,1)S(1)}, bf16[2,256,768]{2,1,0:T(8,128)(2,1)}, u32[]{:S(2)}) copy-start(bf16[2,256,768]{2,1,0:T(8,128)(2,1)} %param.26) | copy-start | bytes 2359300
  260.7 13.8 %copy-start.83 = (f32[2,256,1536]{2,1,0:T(8,128)S(1)}, f32[2,256,1536]{2,1,0:T(8,128)}, u32[]{:S(2)}) copy-start(f32[2,256,1536]{2,1,0:T(8,128)} %copy-done.82) | copy-start | bytes 9437188
  274.5 4.9 copy-start.78
  281.8 93.5 %reduce-scatter.3.cloned.1.call-start = ((), (), s32[]{:S(2)}) async-start(), calls=%async_computation.6 | async-start | bytes 2359296 | tf_op jit(solution)/shard_map/reduce_scatter | solution.py:321
  281.8 34.4 %copy-start.6 = (bf16[2,256,768]{2,1,0:T(8,128)(2,1)S(1)}, bf16[2,256,768]{2,1,0:T(8,128)(2,1)}, u32[]{:S(2)}) copy-start(bf16[2,256,768]{2,1,0:T(8,128)(2,1)} %all-reduce.19.cloned.1.call-done) | copy-start | bytes 2359300
  281.8 37.0 %copy-start.68 = (f32[2,256]{1,0:T(2,128)S(1)}, f32[2,256]{1,0:T(2,128)}, u32[]{:S(2)}) copy-start(f32[2,256]{1,0:T(2,128)} %copy-done.67) | copy-start | bytes 6148
  281.9 37.0 %copy-start.64 = (f32[2,256]{1,0:T(2,128)S(1)}, f32[2,256]{1,0:T(2,128)}, u32[]{:S(2)}) copy-start(f32[2,256]{1,0:T(2,128)} %copy-done.63) | copy-start | bytes 6148
  316.2 5.4 copy-start.24
  316.2 5.4 copy-start.29
  316.3 5.4 copy-start.50
  316.3 7.0 copy-start.32
  323.3 12.2 %copy-start.11 = (f32[2,256,768]{2,1,0:T(8,128)}, f32[2,256,768]{2,1,0:T(8,128)S(1)}, u32[]{:S(2)}) copy-start(f32[2,256,768]{2,1,0:T(8,128)S(1)} %get-tuple-element.110) | copy-start | bytes 4718596
  337.7 4.9 copy-start.5
  342.6 5.4 copy-start.22
  342.6 5.4 copy-start.54
  348.0 6.9 copy-start.10
  354.6 97.8 %all-reduce.27.cloned.1.call-start = ((), (), s32[]{:S(2)}) async-start(), calls=%async_computation.9 | async-start | bytes 5111808 | tf_op jit(solution)/shard_map/psum | solution.py:334
  354.9 9.6 %copy-start.46 = (bf16[1,3456,128]{2,1,0:T(8,128)(2,1)S(1)}, bf16[1,3456,128]{2,1,0:T(8,128)(2,1)}, u32[]{:S(2)}) copy-start(bf16[1,3456,128]{2,1,0:T(8,128)(2,1)} %fusion.28) | copy-start | bytes 2654212
  364.5 6.9 copy-start.21
  375.0 4.2 copy-start.34
  375.0 4.2 copy-start.44
  379.2 101.7 %reduce-scatter.5.cloned.1.call-start = ((), (), s32[]{:S(2)}) async-start(), calls=%async_computation.7 | async-start | bytes 2359296 | tf_op jit(solution)/shard_map/reduce_scatter | solution.py:256
  381.0 408.2 %all-reduce.25.cloned.1.call-start = ((), (), s32[]{:S(2)}) async-start(), calls=%async_computation.8 | async-start | bytes 31850496 | tf_op jit(solution)/shard_map/psum | solution.py:345
  382.6 5.4 copy-start.30
  382.6 5.4 copy-start.51
  382.6 5.4 copy-start.84
  388.0 4.3 copy-start.12
  388.0 4.3 copy-start.41
  388.0 5.8 copy-start.52
  388.0 5.8 copy-start.56
  388.1 5.8 copy-start.58
  388.1 5.8 copy-start.62
  388.1 5.8 copy-start.76
  455.4 26.6 %copy-start.23 = (bf16[2,256,768]{2,1,0:T(8,128)(2,1)S(1)}, bf16[2,256,768]{2,1,0:T(8,128)(2,1)}, u32[]{:S(2)}) copy-start(bf16[2,256,768]{2,1,0:T(8,128)(2,1)} %get-tuple-element.107) | copy-start | bytes 2359300
  455.5 27.1 %copy-start.66 = (f32[2,256]{1,0:T(2,128)S(1)}, f32[2,256]{1,0:T(2,128)}, u32[]{:S(2)}) copy-start(f32[2,256]{1,0:T(2,128)} %copy-done.65) | copy-start | bytes 6148
  455.5 28.1 %copy-start.74 = (f32[1536]{0:T(1024)S(1)}, f32[1536]{0:T(1024)}, u32[]{:S(2)}) copy-start(f32[1536]{0:T(1024)} %get-tuple-element.203) | copy-start | bytes 18436
  789.3 5.3 copy-start.38
  789.3 6.6 copy-start.45
  795.9 4.5 slice-start
  798.0 4.7 copy-start.1
  (40 other events, 77.4 us)
Sparse Core Ops, SparseCore 0:
  16.9 12.4 all-gather.2
  43.6 35.4 all-reduce.18
  90.3 34.3 all-reduce.20
  281.9 34.3 all-reduce.22
  354.7 9.0 reduce-scatter.2
  379.3 73.0 all-reduce.26
  454.8 26.0 reduce-scatter.4
  487.0 302.2 all-reduce.24
where the time goes:
time: 819 us; the launch traced here: 810 us
  waiting for transfers between devices  392 us (48%)
  blocking collectives  119 us (15%)
  local copies, waits for them, and re-layouts  110 us (13%)
  matrix products  96.8 us (12%)
  other arithmetic  55.1 us (7%)
  starting transfers between devices  19.1 us (2%)
  between operations  18.1 us (2%)
    psum x1, waiting for transfers between devices, body(): lax.psum((grad_gains, grad_shifts, grad_qkv, grad_qv_bias, grad_out_weigh...  207 us
    psum x1, blocking collectives, body(): lax.psum((grad_gains, grad_shifts, grad_qkv, grad_qv_bias, grad_out_weigh...  97.2 us
    psum x2, waiting for transfers between devices, body(): lax.psum(partial_value.astype(jnp.bfloat16), 'tensor').astype(jnp.float32)  66.9 us
    unnamed x326, local copies, waits for them, and re-layouts  65 us
    psum x1, waiting for transfers between devices, body(): lax.psum(jnp.einsum('cise,cde->isd', dproject, qkv_weight, preferred_elem...  55.4 us
    psum x1, waiting for transfers between devices, body(): lax.psum(jnp.einsum('isf,df->isd', dhidden, up_weight, preferred_element_...  26.2 us
    reduce_scatter x1, waiting for transfers between devices, body(): lax.psum_scatter(grad_tconv.astype(jnp.bfloat16), 'tensor', scatter_dimen...  24.6 us
  transfers between devices with their start and end apart: 16, of which 8 were waited for; matrix products, arithmetic and copies ran while one was open for 9% of the time, Pallas kernels for 0%

commit v1 on v0

--- a/solution.py
+++ b/solution.py
@@ -1,10 +1,205 @@
+import functools
+
 import jax
 import jax.numpy as jnp
 from jax import lax
+from jax.experimental import pallas as pl
+from jax.experimental.pallas import tpu as pltpu
 from jax.sharding import PartitionSpec as P
 
 GRID = 8
 HD = 64
+
+MESH = pl.DeviceIdType.MESH
+GROUP = 8
+FAR = 4
+
+
+def place():
+    dp = lax.axis_index("dp")
+    blk = lax.axis_index("blk")
+    tensor = lax.axis_index("tensor")
+    near = lax.rem(dp, 2)
+    far = lax.rem(dp // 2, FAR)
+    first = dp // GROUP * GROUP
+    return (dp, blk, tensor, near, far, first)
+
+
+def peers():
+    dp, blk, tensor, near, far, first = place()
+    core = (dp, 1 - blk, tensor)
+    cross = (dp, blk, 1 - tensor)
+    beside = (first + 2 * far + 1 - near, blk, tensor)
+    along = [(first + 2 * lax.rem(far + step, FAR) + near, blk, tensor) for step in range(1, FAR)]
+    return (core, cross, beside, along)
+
+
+def greet(devices):
+    barrier = pltpu.get_barrier_semaphore()
+    for device in devices:
+        pl.semaphore_signal(barrier, inc=1, device_id=device, device_id_type=MESH)
+    pl.semaphore_wait(barrier, len(devices))
+
+
+def remote(src, dst, send, recv, device):
+    return pltpu.make_async_remote_copy(
+        src_ref=src, dst_ref=dst, send_sem=send, recv_sem=recv, device_id=device,
+        device_id_type=MESH,
+    )
+
+
+def rows_at(start, size):
+    return pl.ds(pl.multiple_of(start, 16), size)
+
+
+def add_into(target, target_at, parts, rows, tile):
+    @pl.loop(0, rows // tile)
+    def _(step):
+        at = step * tile
+        total = None
+        for ref, offset in parts:
+            piece = ref[rows_at(offset + at, tile), :].astype(jnp.float32)
+            total = piece if total is None else total + piece
+        target[rows_at(target_at + at, tile), :] = total.astype(jnp.bfloat16)
+
+
+class Sum:
+    def __init__(self, own, from_core, from_near, from_far, total, send, recv):
+        self.own, self.from_core, self.from_near = own, from_core, from_near
+        self.from_far, self.total = from_far, total
+        self.send, self.recv = send, recv
+        self.rows = own.shape[0]
+        self.half, self.quarter, self.piece = self.rows // 2, self.rows // 4, self.rows // 16
+        dp, self.blk, tensor, self.near, self.far, first = place()
+        self.core, cross, self.beside, self.along = peers()
+        self.tile = 48 if self.piece % 48 == 0 else 32
+        self.waiting = []
+
+    def start(self, index, src, dst, device):
+        copy = remote(src, dst, self.send.at[index], self.recv.at[index], device)
+        copy.start()
+        self.waiting.append(copy)
+        return copy
+
+    def step0(self):
+        self.c0 = self.start(
+            0, self.own.at[rows_at((1 - self.blk) * self.half, self.half)], self.from_core,
+            self.core,
+        )
+
+    def step1(self):
+        self.c0.wait_recv()
+        add_into(
+            self.from_core, 0, [(self.from_core, 0), (self.own, self.blk * self.half)],
+            self.half, self.tile,
+        )
+        self.c1 = self.start(
+            1, self.from_core.at[rows_at((1 - self.near) * self.quarter, self.quarter)],
+            self.from_near, self.beside,
+        )
+
+    def step2(self):
+        self.c1.wait_recv()
+        add_into(
+            self.from_near, 0,
+            [(self.from_near, 0), (self.from_core, self.near * self.quarter)],
+            self.quarter, self.tile,
+        )
+        self.c2 = []
+        for step in range(1, FAR):
+            whose = lax.rem(self.far + step, FAR)
+            self.c2.append(
+                self.start(
+                    1 + step, self.from_near.at[rows_at(whose * self.piece, self.piece)],
+                    self.from_far.at[step - 1], self.along[step - 1],
+                )
+            )
+
+    def step3(self):
+        for copy in self.c2:
+            copy.wait_recv()
+        self.base = self.blk * self.half + self.near * self.quarter
+        at = self.base + self.far * self.piece
+        add_into(
+            self.total, at,
+            [(self.from_near, self.far * self.piece)]
+            + [(self.from_far.at[step], 0) for step in range(FAR - 1)],
+            self.piece, self.tile,
+        )
+        self.c3 = []
+        for step in range(1, FAR):
+            where = self.total.at[rows_at(at, self.piece)]
+            self.c3.append(self.start(1 + FAR - 1 + step, where, where, self.along[step - 1]))
+
+    def step4(self):
+        for copy in self.c3:
+            copy.wait_recv()
+        where = self.total.at[rows_at(self.base, self.quarter)]
+        self.c4 = self.start(2 * FAR, where, where, self.beside)
+
+    def step5(self):
+        self.c4.wait_recv()
+        where = self.total.at[rows_at(self.blk * self.half, self.half)]
+        self.c5 = self.start(2 * FAR + 1, where, where, self.core)
+
+    def step6(self):
+        self.c5.wait_recv()
+        for copy in self.waiting:
+            copy.wait_send()
+
+
+COPIES = 2 * FAR + 2
+
+
+def sum_scratch(rows, columns):
+    return [
+        pltpu.VMEM((rows // 2, columns), jnp.bfloat16),
+        pltpu.VMEM((rows // 4, columns), jnp.bfloat16),
+        pltpu.VMEM((FAR - 1, rows // 16, columns), jnp.bfloat16),
+    ]
+
+
+def total_kernel(count, *refs):
+    owns, totals = refs[:count], refs[count : 2 * count]
+    scratch = refs[2 * count :]
+    send, recv = scratch[3 * count :]
+    core, cross, beside, along = peers()
+    greet([core, beside] + along)
+    sums = [
+        Sum(owns[i], *scratch[3 * i : 3 * i + 3], totals[i], send.at[i], recv.at[i])
+        for i in range(count)
+    ]
+    for wave in range(count + 6):
+        for i in range(count):
+            if 0 <= wave - i <= 6:
+                getattr(sums[i], "step" + str(wave - i))()
+
+
+def total_over_group(arrays):
+    count = len(arrays)
+    scratch = []
+    for array in arrays:
+        scratch += sum_scratch(*array.shape)
+    return pl.pallas_call(
+        functools.partial(total_kernel, count),
+        out_shape=[jax.ShapeDtypeStruct(array.shape, jnp.bfloat16) for array in arrays],
+        in_specs=[pl.BlockSpec(memory_space=pltpu.VMEM)] * count,
+        out_specs=[pl.BlockSpec(memory_space=pltpu.VMEM)] * count,
+        scratch_shapes=scratch
+        + [pltpu.SemaphoreType.DMA((count, COPIES)), pltpu.SemaphoreType.DMA((count, COPIES))],
+        name="weight_sums",
+        compiler_params=pltpu.CompilerParams(
+            collective_id=0, has_side_effects=True, vmem_limit_bytes=60 * 2**20
+        ),
+    )(*arrays)
+
+
+def swap(value, axis):
+    return lax.ppermute(value, axis, [(0, 1), (1, 0)])
+
+
+def pair_sum(value):
+    return value.astype(jnp.float32) + swap(value, "tensor").astype(jnp.float32)
 
 
 def extended(block, sides, width):
@@ -88,9 +283,8 @@
 
 
 def channel_sums(first_term, second_term):
-    return lax.psum(
-        (jnp.sum(first_term, axis=(1, 2, 3)), jnp.sum(second_term, axis=(1, 2, 3))), "blk"
-    )
+    sums = jnp.stack([jnp.sum(first_term, axis=(1, 2, 3)), jnp.sum(second_term, axis=(1, 2, 3))])
+    return sums + swap(sums, "blk")
 
 
 def norm_forward(level, voxel_valid, voxel_count):
@@ -191,7 +385,7 @@
     )
     partial_value = lax.optimization_barrier(partial_value.astype(jnp.bfloat16)).astype(jnp.float32)
     middle = inputs + (
-        lax.psum(partial_value.astype(jnp.bfloat16), "tensor").astype(jnp.float32) + shifts[2]
+        pair_sum(partial_value.astype(jnp.bfloat16)) + shifts[2]
     )
     normed_two = layer_norm(middle, norm_gains[1], shifts[1]).astype(jnp.bfloat16)
     hidden = (
@@ -204,7 +398,7 @@
     )
     partial_value = lax.optimization_barrier(partial_value.astype(jnp.bfloat16)).astype(jnp.float32)
     block_out = middle + (
-        lax.psum(partial_value.astype(jnp.bfloat16), "tensor").astype(jnp.float32) + shifts[3]
+        pair_sum(partial_value.astype(jnp.bfloat16)) + shifts[3]
     )
     out_low = block_out.astype(jnp.bfloat16)
     per_device = item_count // lax.axis_size("tensor")
@@ -252,14 +446,19 @@
     grad_tconv = jnp.einsum("isd,isk->dk", tapped, dlifted, preferred_element_type=jnp.float32)
     dtapped = jnp.einsum("isk,dk->isd", dlifted, tconv_weight, preferred_element_type=jnp.float32)
     grad_kernel_pair = jnp.stack([grad_kernel_one, grad_kernel_two])
-    dec_parts = (
-        lax.psum_scatter(
-            grad_tconv.astype(jnp.bfloat16), "tensor", scatter_dimension=1, tiled=True
-        ).astype(jnp.float32),
-        lax.psum_scatter(
-            grad_kernel_pair.astype(jnp.bfloat16), "tensor", scatter_dimension=2, tiled=True
-        ).astype(jnp.float32),
-    )
+    low = jnp.bfloat16
+    mine = lax.axis_index("tensor")
+    tconv_halves = grad_tconv.astype(low).reshape(768, 2, 512)
+    kernel_halves = (
+        grad_kernel_pair.astype(low).reshape(2, 3456, 2, 64).transpose(2, 1, 0, 3)
+        .reshape(2, 3456, 128)
+    )
+    keep = lax.dynamic_index_in_dim(tconv_halves, mine, 1, False)
+    give = lax.dynamic_index_in_dim(tconv_halves, 1 - mine, 1, False)
+    tconv_part = (keep + swap(give, "tensor")).astype(low)
+    keep = lax.dynamic_index_in_dim(kernel_halves, mine, 0, False)
+    give = lax.dynamic_index_in_dim(kernel_halves, 1 - mine, 0, False)
+    kernel_part = jnp.pad((keep + swap(give, "tensor")).astype(low), ((0, 128), (0, 0)))
     dtap_all = lax.all_gather(dtapped.astype(jnp.bfloat16), "tensor", axis=0, tiled=True).astype(
         dtapped.dtype
     )
@@ -272,12 +471,11 @@
     dhidden = gelu_back(dactive)[0].astype(jnp.bfloat16)
     grad_up_bias = jnp.sum(dhidden.astype(jnp.float32), axis=(0, 1))
     grad_up = jnp.einsum("isd,isf->df", normed_two, dhidden, preferred_element_type=jnp.float32)
-    dnormed_two = lax.psum(
+    dnormed_two = pair_sum(
         jnp.einsum("isf,df->isd", dhidden, up_weight, preferred_element_type=jnp.float32).astype(
             jnp.bfloat16
-        ),
-        "tensor",
-    ).astype(jnp.float32)
+        )
+    )
     norm_value, norm_back_two = jax.vjp(layer_norm, middle, norm_gains[1], shifts[1])
     dmid_norm, grad_gain_one, grad_shift_one = norm_back_two(dnormed_two)
     dmiddle = dout + dmid_norm
@@ -331,48 +529,48 @@
         ]
     )
     grad_qkv = jnp.einsum("isd,cise->cde", normed_one, dproject, preferred_element_type=jnp.float32)
-    dnormed_one = lax.psum(
+    dnormed_one = pair_sum(
         jnp.einsum(
             "cise,cde->isd", dproject, qkv_weight, preferred_element_type=jnp.float32
-        ).astype(jnp.bfloat16),
-        "tensor",
-    ).astype(jnp.float32)
+        ).astype(jnp.bfloat16)
+    )
     norm_first, norm_back_one = jax.vjp(layer_norm, inputs, norm_gains[0], shifts[0])
     din_norm, grad_gain_zero, grad_shift_zero = norm_back_one(dnormed_one)
     grad_input = (dmiddle + din_norm).astype(jnp.bfloat16)
     grad_gains = jnp.stack([grad_gain_zero, grad_gain_one])
     grad_shifts = jnp.stack([grad_shift_zero, grad_shift_one, grad_shift_two, grad_shift_three])
-    summed_all = lax.psum(
-        (
-            grad_gains,
-            grad_shifts,
-            grad_qkv,
-            grad_qv_bias,
-            grad_out_weight,
-            grad_up,
-            grad_up_bias,
-            grad_down,
-            dec_parts[0],
-            dec_parts[1],
-        ),
-        ("dp", "blk"),
-    )
-    summed = summed_all[:8]
-    dec_final = summed_all[8:]
+    small = lax.psum((grad_gains, grad_shifts, grad_qv_bias, grad_up_bias), ("dp", "blk"))
+    big = total_over_group(
+        [
+            kernel_part,
+            tconv_part,
+            grad_down.astype(low),
+            grad_up.astype(low),
+            jnp.concatenate([grad_out_weight[:, :384], grad_out_weight[:, 384:]]).astype(low),
+            grad_qkv.astype(low).reshape(2304, 384),
+        ]
+    )
+    big = [array.astype(jnp.float32) for array in big]
+    groups = lax.axis_size("dp") // GROUP
+    if groups > 1:
+        same = [[part * GROUP + i for part in range(groups)] for i in range(GROUP)]
+        big = [lax.psum(array, "dp", axis_index_groups=same) for array in big]
+    sum_kernel, sum_tconv, sum_down, sum_up, sum_out, sum_qkv = big
+    sum_kernel = sum_kernel[:3456].reshape(3456, 2, 64).transpose(1, 0, 2)
     return (
         out_low,
         decoded,
         grad_input,
-        summed[0],
-        summed[1],
-        summed[2],
-        summed[3],
-        summed[4],
-        summed[5],
-        summed[6],
-        summed[7],
-        dec_final[0],
-        dec_final[1],
+        small[0],
+        small[1],
+        sum_qkv.reshape(3, 768, 384),
+        small[2],
+        jnp.concatenate([sum_out[:384], sum_out[384:]], axis=1),
+        sum_up,
+        small[3],
+        sum_down,
+        sum_tconv,
+        sum_kernel,
     )
 
 

time: 819 us -> 593 us (0.72)
  waiting for transfers between devices: 392 us -> 43.4 us
  Pallas kernels: 0 us -> 129 us
  blocking collectives: 119 us -> 74.7 us
  local copies, waits for them, and re-layouts: 110 us -> 130 us
  other arithmetic: 55.1 us -> 74.2 us
  matrix products: 96.8 us -> 84.6 us
  starting transfers between devices: 19.1 us -> 28.4 us
    psum x5 -> x0, waiting for transfers between devices: 355 us -> none  [the longest x1 207 us: body(): lax.psum((grad_gains, grad_shifts, grad_qkv, grad_qv_bias, grad_out_weigh...]
    pallas_call x0 -> x1, Pallas kernels: none -> 129 us  [total_over_group(): pl.pallas_call(functools.partial(total_kernel, count), out_shape=[jax.Sha...]
    psum x5 -> x1, blocking collectives: 107 us -> 64.2 us  [body(): lax.psum((grad_gains, grad_shifts, grad_qv_bias, grad_up_bias), ('dp', 'b...]
    ppermute x0 -> x10, waiting for transfers between devices: none -> 32.3 us  [swap(): return lax.ppermute(value, axis, [(0, 1), (1, 0)])]
    reduce_scatter x1 -> x0, waiting for transfers between devices: 24.6 us -> none  [body(): lax.psum_scatter(grad_tconv.astype(jnp.bfloat16), 'tensor', scatter_dimen...]
    dynamic_slice x0 -> x4, local copies, waits for them, and re-layouts: none -> 12.2 us  [the longest x1 6.42 us: body(): keep = lax.dynamic_index_in_dim(tconv_halves, mine, 1, False)]
    unnamed x326 -> x367, local copies, waits for them, and re-layouts: 65 us -> 55.3 us
    ppermute x0 -> x10, starting transfers between devices: none -> 8.21 us  [swap(): return lax.ppermute(value, axis, [(0, 1), (1, 0)])]
  transfers between devices with their start and end apart: 16 -> 20, of which waited for: 8 -> 3; matrix products, arithmetic and copies ran while one was open for 9% -> 23% of each run, Pallas kernels for 0% -> 22%
where the time goes in v1:
time: 593 us; the launch traced here: 582 us
  local copies, waits for them, and re-layouts  130 us (22%)
  Pallas kernels  129 us (22%)
  matrix products  84.6 us (14%)
  blocking collectives  74.7 us (13%)
  other arithmetic  74.2 us (13%)
  waiting for transfers between devices  43.4 us (7%)
  starting transfers between devices  28.4 us (5%)
  between operations  17.6 us (3%)
    pallas_call x1, Pallas kernels, total_over_group(): pl.pallas_call(functools.partial(total_kernel, count), out_shape=[jax.Sha...  129 us
    psum x1, blocking collectives, body(): lax.psum((grad_gains, grad_shifts, grad_qv_bias, grad_up_bias), ('dp', 'b...  64.2 us
    unnamed x367, local copies, waits for them, and re-layouts  55.3 us
    ppermute x10, waiting for transfers between devices, swap(): return lax.ppermute(value, axis, [(0, 1), (1, 0)])  32.3 us
    ppermute x4, starting transfers between devices, extended(): lax.ppermute(lax.slice_in_dim(block, block.shape[dim] - width, None, axis...  15 us
    dot_general x2, matrix products, conv_input_grad(): jnp.dot(columns_of(with_rims(dlevel)), flipped, preferred_element_type=jn...  12.2 us
  transfers between devices with their start and end apart: 20, of which 3 were waited for; matrix products, arithmetic and copies ran while one was open for 23% of the time, Pallas kernels for 22%

profile of v1, /device:TPU:0, one launch (start us, length us, event | category | flops | bytes accessed | tf_op | source)
XLA Modules:
  0.0 582.4 jit_solution(3906580600098780100)
XLA Ops:
  12.0 3.1 fusion.61
  18.8 11.0 %all-gather.3.cloned.1.call-done = bf16[2,2,512,384]{3,2,0,1:T(8,128)(2,1)} async-done(((bf16[2,2,256,384]{3,2,0,1:T(8,128)(2,1)}), bf16[2,2,512,384]{3,2,0,1:T(8,128)(2,1)}) %all-gather.3.cloned.1.call-update) | async-done | bytes 1572880 | tf_op jit(solution)/shard_map/all_gather | solution.py:356
  29.8 2.7 fusion.173
  32.5 2.3 copy.79
  34.7 2.3 copy.81
  37.0 2.6 fusion.180
  41.2 2.2 fusion.95
  45.9 18.0 %collective-permute-done = bf16[2,256,768]{2,1,0:T(8,128)(2,1)S(1)} collective-permute-done((bf16[2,256,768]{2,1,0:T(8,128)(2,1)S(1)}, bf16[2,256,768]{2,1,0:T(8,128)(2,1)S(1)}, u32[]{:S(2)}, u32[]{:S(2)}) %collective-permute-start) | collective-permute-done | bytes 786464 | tf_op jit(solution)/shard_map/ppermute | solution.py:198
  67.6 2.0 fusion.76
  71.5 2.6 copy.124
  74.3 14.3 %collective-permute-done.1 = bf16[2,256,768]{2,1,0:T(8,128)(2,1)} collective-permute-done((bf16[2,256,768]{2,1,0:T(8,128)(2,1)S(1)}, bf16[2,256,768]{2,1,0:T(8,128)(2,1)}, u32[]{:S(2)}, u32[]{:S(2)}) %collective-permute-start.1) | collective-permute-done | bytes 786464 | tf_op jit(solution)/shard_map/ppermute | solution.py:198
  91.4 2.0 convolution_bitcast_fusion.1
  97.1 4.4 collective-permute-start.2
  114.6 5.0 copy-done.71
  119.7 3.5 constant_dynamic-update-slice_fusion.54
  127.0 4.1 multiply_reduce_fusion.4
  134.2 3.2 collective-permute-start.5
  146.7 5.0 copy-done.72
  151.8 3.3 constant_dynamic-update-slice_fusion.81
  159.0 4.2 multiply_reduce_fusion.3
  167.8 2.2 copy.92
  170.0 2.2 copy.90
  172.2 1.9 multiply_convert_fusion.3
  176.8 3.7 collective-permute-start.9
  181.2 3.6 dot_general.140
  193.5 5.4 copy-done.73
  199.0 7.8 %fusion.163 = (f32[128]{0:T(128)S(1)}, f32[128]{0:T(128)S(1)}, f32[8,16,16,128]{3,2,1,0:T(8,128)S(1)}) fusion(f32[128]{0:T(128)S(1)} %copy-done.66, f32[128]{0:T(128)S(1)} %copy-done.69, f32[2048,128]{1,0:T(8,128)S(1)} %get-tuple-element.157, f32[8,16,16,128]{3,2,1,0:T(8,128)S(1)} %bitcast.359, f32[8,16,16]{2,1,0:T(8,128)S(1)} %copy.87, ...), kind=kOutput, calls=%fused_computation.435 | convolution fusion | flops 1816395520 | bytes 18196480 | tf_op jit(solution)/shard_map/dot_general | solution.py:318
  207.1 3.1 fusion.28
  213.9 3.7 collective-permute-start.12
  217.6 3.3 dot_general.135
  220.9 7.5 %fusion.25 = bf16[1,3456,2,64]{1,3,2,0:T(8,128)(2,1)S(1)} fusion(bf16[1,8,16,16,3456]{4,3,2,1,0:T(8,128)(2,1)} %get-tuple-element.83, bf16[2,64,8,16,16]{1,0,4,3,2:T(2,128)(2,1)} %dot_general.135), kind=kOutput, calls=%fused_computation.25 | convolution fusion | flops 1812381696 | bytes 15564800 | tf_op jit(solution)/shard_map/rk,rc->kc/dot_general | solution.py:438
  238.2 4.4 fusion.89
  244.2 10.5 %all-gather = bf16[512,768]{1,0:T(8,128)(2,1)S(1)} all-gather(bf16[256,768]{1,0:T(8,128)(2,1)S(1)} %convolution_convert_fusion.4), channel_id=2, replica_groups=mesh['dp'=8,'blk'=2,'tensor'=2] {'tensor'}, dimensions={0}, use_global_device_ids=true | all-gather | bytes 1179648 | tf_op jit(solution)/shard_map/all_gather | solution.py:462
  254.7 3.7 convert_reduce_fusion
  258.5 2.3 fusion.73
  263.8 2.2 copy.102
  266.3 2.2 copy.101
  268.5 2.8 convolution_convert_fusion.1
  271.3 3.9 reshape.769
  275.2 6.4 %constant_dynamic-slice_fusion.1 = (bf16[768,1,512]{2,1,0:T(2,128)(2,1)}, bf16[768,1,512]{2,1,0:T(2,128)(2,1)S(1)}) fusion(bf16[768,2,512]{2,1,0:T(2,128)(2,1)} %reshape.769, s32[]{:T(128)S(6)} %select_n.79, s32[]{:T(128)S(6)} %select_n.83), kind=kLoop, calls=%fused_computation.391 | loop fusion | bytes 3145736 | tf_op jit(solution)/shard_map/jit(dynamic_index_in_dim)/dynamic_slice | solution.py:456
  284.5 2.7 multiply_reduce_fusion
  287.2 2.1 fusion.166
  294.9 3.8 convolution_convert_fusion
  298.7 4.8 fusion.79
  303.5 2.3 copy.96
  305.8 5.0 fusion.8
  310.9 3.7 fusion.10
  317.9 2.3 copy.95
  320.2 2.7 pad_maximum_fusion
  323.0 5.0 bitcast_convert_fusion.refs_3_
  328.1 3.5 bitcast_convert_fusion.1.refs_2_
  338.0 2.7 fusion.120.refs_1_
  343.3 3.9 bitcast_convert_fusion.3
  347.5 3.7 fusion.69
  351.1 3.8 copy.108
  355.0 129.4 %weight_sums.1 = (bf16[3584,128]{1,0:T(8,128)(2,1)}, bf16[768,512]{1,0:T(8,128)(2,1)}, bf16[1536,768]{1,0:T(8,128)(2,1)}, bf16[768,1536]{1,0:T(8,128)(2,1)}, bf1...) custom-call(bf16[3584,128]{1,0:T(8,128)(2,1)} %pad.21.refs_0_, bf16[768,512]{1,0:T(8,128)(2,1)} %fusion.120.refs_1_, ...), custom_call_target="tpu_custom_call" | custom-call | tf_op jit(solution)/shard_map/weight_sums/pallas_call | solution.py:183
  484.4 2.7 slice_convert_fusion
  488.2 3.6 convert.38
  491.9 2.8 convert_element_type.318
  494.7 2.5 convert_element_type.320
  498.6 2.7 copy.109
  505.7 2.3 fusion.66
  508.1 2.9 convert_reduce_fusion.2
  511.1 64.2 %all-reduce.5 = (f32[2,768]{1,0:T(2,128)}, f32[4,768]{1,0:T(4,128)}, f32[2,384]{1,0:T(2,128)}, f32[1536]{0:T(1024)}) all-reduce(f32[2,768]{1,0:T(2,128)S(1)} %pad_maximum_fusion.16, f32[4,768]{1,0:T(4,128)S(1)} %pad_maximum_fusion.15, f32[2,384]{1,0:T(2,128)S(1)} %pad_maximum_fusion.17, ...), channel_id=1, replica_groups=mesh['dp'=8,'blk'=2,'tensor'=2] {'dp','blk'}, use_global_device_ids=true, to_apply=%region_23.24 | all-reduce | flops 6912 | bytes 55296 | tf_op jit(solution)/shard_map/psum | solution.py:542
  (518 shorter events, 119.0 us)
Async XLA Ops:
  7.2 60.4 %copy-start = (bf16[1536,768]{1,0:T(8,128)(2,1)S(1)}, bf16[1536,768]{1,0:T(8,128)(2,1)}, u32[]{:S(2)}) copy-start(bf16[1536,768]{1,0:T(8,128)(2,1)} %param.23) | copy-start | bytes 7077892
  7.2 22.6 %all-gather.3.cloned.1.call-start = ((), (), s32[]{:S(2)}) async-start(), calls=%async_computation.1 | async-start | bytes 2359296 | tf_op jit(solution)/shard_map/all_gather | solution.py:356
  8.7 7.4 %copy-start.57 = (f32[2,256]{1,0:T(2,128)}, f32[2,256]{1,0:T(2,128)S(1)}, u32[]{:S(2)}) copy-start(f32[2,256]{1,0:T(2,128)S(1)} %broadcast_multiply_fusion.1) | copy-start | bytes 6148
  12.0 53.4 %copy-start.59 = (f32[768]{0:T(1024)}, f32[768]{0:T(1024)S(1)}, u32[]{:S(2)}) copy-start(f32[768]{0:T(1024)S(1)} %get-tuple-element.165) | copy-start | bytes 9220
  12.0 53.4 %copy-start.97 = (f32[768]{0:T(1024)}, f32[768]{0:T(1024)S(1)}, u32[]{:S(2)}) copy-start(f32[768]{0:T(1024)S(1)} %get-tuple-element.42) | copy-start | bytes 9220
  17.1 326.2 %reduce-scatter.2.cloned.1.call-start = ((), (), s32[]{:S(2)}) async-start(), calls=%async_computation.2 | async-start | bytes 2359296 | tf_op jit(solution)/shard_map/reduce_scatter | solution.py:519
  18.6 21.0 %copy-start.19 = (f32[1,2,256,384]{2,3,1,0:T(8,128)}, f32[1,2,256,384]{2,3,1,0:T(8,128)S(1)}, u32[]{:S(2)}) copy-start(f32[1,2,256,384]{2,3,1,0:T(8,128)S(1)} %copy.80) | copy-start | bytes 2359300
  18.7 20.9 %copy-start.52 = (f32[6,64]{1,0:T(8,128)}, f32[6,64]{1,0:T(8,128)S(1)}, u32[]{:S(2)}) copy-start(f32[6,64]{1,0:T(8,128)S(1)} %add.310) | copy-start | bytes 4612
  41.2 22.7 %copy-start.7 = (bf16[2,256,768]{2,1,0:T(8,128)(2,1)S(1)}, bf16[2,256,768]{2,1,0:T(8,128)(2,1)}, u32[]{:S(2)}) copy-start(bf16[2,256,768]{2,1,0:T(8,128)(2,1)} %param.14) | copy-start | bytes 2359300
  43.4 24.1 %copy-start.37 = (bf16[2,6,64,256]{3,2,1,0:T(8,128)(2,1)}, bf16[2,6,64,256]{3,2,1,0:T(8,128)(2,1)S(1)}, u32[]{:S(2)}) copy-start(bf16[2,6,64,256]{3,2,1,0:T(8,128)(2,1)S(1)} %fusion.95) | copy-start | bytes 1179652
  43.4 22.6 %copy-start.99 = (bf16[768,1536]{1,0:T(8,128)(2,1)S(1)}, bf16[768,1536]{1,0:T(8,128)(2,1)}, u32[]{:S(2)}) copy-start(bf16[768,1536]{1,0:T(8,128)(2,1)} %param.21) | copy-start | bytes 7077892
  43.4 22.6 %copy-start.101 = (f32[1536]{0:T(1024)S(1)}, f32[1536]{0:T(1024)}, u32[]{:S(2)}) copy-start(f32[1536]{0:T(1024)} %param.22) | copy-start | bytes 18436
  44.1 19.8 %collective-permute-start = (bf16[2,256,768]{2,1,0:T(8,128)(2,1)S(1)}, bf16[2,256,768]{2,1,0:T(8,128)(2,1)S(1)}, u32[]{:S(2)}, u32[]{:S(2)}) collective-permute-start(bf16[2,256,768]{2,1,0:T(8,128)(2,1)S(1)} %convolution_convert_fusion.2), channel_id=1, source_target_pairs={{0,1},{1,0},{2,3},{3,2},{4,5},{5,4},{6,7},{7,6},{8,9},{9,8},{10,11... | collective-permute-start | bytes 2359304 | tf_op jit(solution)/shard_map/ppermute | solution.py:198
  69.5 19.1 %collective-permute-start.1 = (bf16[2,256,768]{2,1,0:T(8,128)(2,1)S(1)}, bf16[2,256,768]{2,1,0:T(8,128)(2,1)}, u32[]{:S(2)}, u32[]{:S(2)}) collective-permute-start(bf16[2,256,768]{2,1,0:T(8,128)(2,1)S(1)} %fusion.76), channel_id=1, source_target_pairs={{0,1},{1,0},{2,3},{3,2},{4,5},{5,4},{6,7},{7,6},{8,9},{9,8},{10,11... | collective-permute-start | bytes 2359304 | tf_op jit(solution)/shard_map/ppermute | solution.py:198
  95.8 8.1 %collective-permute-start.3 = (bf16[1,1,16,16,128]{4,3,2,1,0:T(8,128)(2,1)}, bf16[1,1,16,16,128]{4,3,2,1,0:T(8,128)(2,1)}, u32[]{:S(2)}, u32[]{:S(2)}) collective-permute-start(bf16[1,1,16,16,128]{4,3,2,1,0:T(8,128)(2,1)} %get-tuple-element.148), channel_id=1, source_target_pairs={{2,0},{3,1},{6,4},{7,5},{10,8},{11,9},{14,12},{15,13},{18,16},{19,... | collective-permute-start | bytes 196616 | tf_op jit(solution)/shard_map/ppermute | solution.py:213
  97.1 6.8 %collective-permute-start.2 = (bf16[1,1,16,16,128]{4,3,2,1,0:T(8,128)(2,1)}, bf16[1,1,16,16,128]{4,3,2,1,0:T(8,128)(2,1)}, u32[]{:S(2)}, u32[]{:S(2)}) collective-permute-start(bf16[1,1,16,16,128]{4,3,2,1,0:T(8,128)(2,1)} %get-tuple-element.147), channel_id=1, source_target_pairs={{0,2},{1,3},{4,6},{5,7},{8,10},{9,11},{12,14},{13,15},{16,18},{17,... | collective-permute-start | bytes 196616 | tf_op jit(solution)/shard_map/ppermute | solution.py:210
  131.1 1.3 collective-permute-start.4
  132.5 24.3 %copy-start.65 = (f32[128]{0:T(128)}, f32[128]{0:T(128)S(1)}, u32[]{:S(2)}) copy-start(f32[128]{0:T(128)S(1)} %get-tuple-element.66) | copy-start | bytes 1540
  132.5 24.3 %copy-start.68 = (f32[128]{0:T(128)}, f32[128]{0:T(128)S(1)}, u32[]{:S(2)}) copy-start(f32[128]{0:T(128)S(1)} %get-tuple-element.67) | copy-start | bytes 1540
  132.9 6.1 %collective-permute-start.6 = (bf16[1,1,16,16,128]{4,3,2,1,0:T(8,128)(2,1)S(1)}, bf16[1,1,16,16,128]{4,3,2,1,0:T(8,128)(2,1)S(1)}, u32[]{:S(2)}, u32[]{:S(2)}) collective-permute-start(bf16[1,1,16,16,128]{4,3,2,1,0:T(8,128)(2,1)S(1)} %get-tuple-element.146), channel_id=1, source_target_pairs={{2,0},{3,1},{6,4},{7,5},{10,8},{11,9},{14,12},{15,13},{18,16},{19,... | collective-permute-start | bytes 196616 | tf_op jit(solution)/shard_map/ppermute | solution.py:213
  134.2 4.8 collective-permute-start.5
  163.2 1.2 collective-permute-start.7
  166.3 5.8 collective-permute-start.8
  175.5 9.3 %collective-permute-start.10 = (bf16[1,1,16,16,128]{4,3,2,1,0:T(8,128)(2,1)}, bf16[1,1,16,16,128]{4,3,2,1,0:T(8,128)(2,1)S(1)}, u32[]{:S(2)}, u32[]{:S(2)}) collective-permute-start(bf16[1,1,16,16,128]{4,3,2,1,0:T(8,128)(2,1)} %get-tuple-element.144), channel_id=1, source_target_pairs={{2,0},{3,1},{6,4},{7,5},{10,8},{11,9},{14,12},{15,13},{18,16},{19,... | collective-permute-start | bytes 196616 | tf_op jit(solution)/shard_map/ppermute | solution.py:213
  176.8 8.1 %collective-permute-start.9 = (bf16[1,1,16,16,128]{4,3,2,1,0:T(8,128)(2,1)}, bf16[1,1,16,16,128]{4,3,2,1,0:T(8,128)(2,1)}, u32[]{:S(2)}, u32[]{:S(2)}) collective-permute-start(bf16[1,1,16,16,128]{4,3,2,1,0:T(8,128)(2,1)} %get-tuple-element.143), channel_id=1, source_target_pairs={{0,2},{1,3},{4,6},{5,7},{8,10},{9,11},{12,14},{13,15},{16,18},{17,... | collective-permute-start | bytes 196616 | tf_op jit(solution)/shard_map/ppermute | solution.py:210
  190.7 8.3 %copy-start.45 = (bf16[27,128,128]{2,1,0:T(8,128)(2,1)S(1)}, bf16[27,128,128]{2,1,0:T(8,128)(2,1)}, u32[]{:S(2)}) copy-start(bf16[27,128,128]{2,1,0:T(8,128)(2,1)} %copy.90) | copy-start | bytes 2654212
  190.7 8.3 %copy-start.66 = (f32[128]{0:T(128)S(1)}, f32[128]{0:T(128)}, u32[]{:S(2)}) copy-start(f32[128]{0:T(128)} %copy-done.65) | copy-start | bytes 1540
  190.7 8.3 %copy-start.69 = (f32[128]{0:T(128)S(1)}, f32[128]{0:T(128)}, u32[]{:S(2)}) copy-start(f32[128]{0:T(128)} %copy-done.68) | copy-start | bytes 1540
  192.9 14.0 %slice-start = ((s8[14155776]{0:T(1024)(128)(4,1)}), s8[4194304]{0:T(1024)(128)(4,1)S(1)}, s32[]{:S(2)}) async-start(s8[14155776]{0:T(1024)(128)(4,1)} %bitcast.451), calls=%async_computation.3 | async-start | bytes 8388608
  198.9 7.9 %copy-start.42 = (bf16[2,64,8,16,16]{1,0,4,3,2:T(2,128)(2,1)S(1)}, bf16[2,64,8,16,16]{1,0,4,3,2:T(2,128)(2,1)}, u32[]{:S(2)}) copy-start(bf16[2,64,8,16,16]{1,0,4,3,2:T(2,128)(2,1)} %dot_general.140) | copy-start | bytes 1572868
  198.9 7.9 %slice-start.1 = ((s8[14155776]{0:T(1024)(128)(4,1)}), s8[4194304]{0:T(1024)(128)(4,1)S(1)}, s32[]{:S(2)}) async-start(s8[14155776]{0:T(1024)(128)(4,1)} %bitcast.451), calls=%async_computation.4 | async-start | bytes 8388608
  199.0 7.9 %slice-start.2 = ((s8[14155776]{0:T(1024)(128)(4,1)}), s8[4194304]{0:T(1024)(128)(4,1)S(1)}, s32[]{:S(2)}) async-start(s8[14155776]{0:T(1024)(128)(4,1)} %bitcast.451), calls=%async_computation.5 | async-start | bytes 8388608
  199.0 8.2 %slice-start.3 = ((s8[14155776]{0:T(1024)(128)(4,1)}), s8[1572864]{0:T(1024)(128)(4,1)S(1)}, s32[]{:S(2)}) async-start(s8[14155776]{0:T(1024)(128)(4,1)} %bitcast.451), calls=%async_computation.6 | async-start | bytes 3145728
  206.8 3.5 collective-permute-start.11
  212.6 16.1 %collective-permute-start.13 = (bf16[1,1,16,16,128]{4,3,2,1,0:T(8,128)(2,1)}, bf16[1,1,16,16,128]{4,3,2,1,0:T(8,128)(2,1)S(1)}, u32[]{:S(2)}, u32[]{:S(2)}) collective-permute-start(bf16[1,1,16,16,128]{4,3,2,1,0:T(8,128)(2,1)} %get-tuple-element.142), channel_id=1, source_target_pairs={{2,0},{3,1},{6,4},{7,5},{10,8},{11,9},{14,12},{15,13},{18,16},{19,... | collective-permute-start | bytes 196616 | tf_op jit(solution)/shard_map/ppermute | solution.py:213
  213.9 14.8 %collective-permute-start.12 = (bf16[1,1,16,16,128]{4,3,2,1,0:T(8,128)(2,1)}, bf16[1,1,16,16,128]{4,3,2,1,0:T(8,128)(2,1)}, u32[]{:S(2)}, u32[]{:S(2)}) collective-permute-start(bf16[1,1,16,16,128]{4,3,2,1,0:T(8,128)(2,1)} %get-tuple-element.141), channel_id=1, source_target_pairs={{0,2},{1,3},{4,6},{5,7},{8,10},{9,11},{12,14},{13,15},{16,18},{17,... | collective-permute-start | bytes 196616 | tf_op jit(solution)/shard_map/ppermute | solution.py:210
  220.9 7.5 %copy-start.43 = (bf16[1,3456,2,64]{1,3,2,0:T(8,128)(2,1)S(1)}, bf16[1,3456,2,64]{1,3,2,0:T(8,128)(2,1)}, u32[]{:S(2)}) copy-start(bf16[1,3456,2,64]{1,3,2,0:T(8,128)(2,1)} %fusion.28) | copy-start | bytes 2654212
  238.2 16.5 %copy-start.27 = (bf16[2,256,768]{2,1,0:T(8,128)(2,1)S(1)}, bf16[2,256,768]{2,1,0:T(8,128)(2,1)}, u32[]{:S(2)}) copy-start(bf16[2,256,768]{2,1,0:T(8,128)(2,1)} %param.26) | copy-start | bytes 2359300
  238.2 16.5 %copy-start.104 = (f32[2,256,1536]{2,1,0:T(8,128)S(1)}, f32[2,256,1536]{2,1,0:T(8,128)}, u32[]{:S(2)}) copy-start(f32[2,256,1536]{2,1,0:T(8,128)} %copy-done.103) | copy-start | bytes 9437188
  254.7 73.3 %copy-start.22 = (bf16[512,768]{1,0:T(8,128)(2,1)}, bf16[512,768]{1,0:T(8,128)(2,1)S(1)}, u32[]{:S(2)}) copy-start(bf16[512,768]{1,0:T(8,128)(2,1)S(1)} %all-gather) | copy-start | bytes 2359300
  258.5 10.1 %copy-start.41 = (bf16[1,256,768]{2,1,0:T(8,128)(2,1)S(1)}, bf16[1,256,768]{2,1,0:T(8,128)(2,1)}, u32[]{:S(2)}) copy-start(bf16[1,256,768]{2,1,0:T(8,128)(2,1)} %copy-done.40) | copy-start | bytes 1179652
  260.8 23.7 %collective-permute-start.14 = (bf16[2,256,768]{2,1,0:T(8,128)(2,1)}, bf16[2,256,768]{2,1,0:T(8,128)(2,1)}, u32[]{:S(2)}, u32[]{:S(2)}) collective-permute-start(bf16[2,256,768]{2,1,0:T(8,128)(2,1)} %fusion.73), channel_id=1, source_target_pairs={{0,1},{1,0},{2,3},{3,2},{4,5},{5,4},{6,7},{7,6},{8,9},{9,8},{10,11... | collective-permute-start | bytes 2359304 | tf_op jit(solution)/shard_map/ppermute | solution.py:198
  266.0 74.7 %collective-permute-start.16 = (bf16[3456,128]{1,0:T(8,128)(2,1)}, bf16[3456,128]{1,0:T(8,128)(2,1)}, u32[]{:S(2)}, u32[]{:S(2)}) collective-permute-start(bf16[3456,128]{1,0:T(8,128)(2,1)} %bitcast.444), channel_id=1, source_target_pairs={{0,1},{1,0},{2,3},{3,2},{4,5},{5,4},{6,7},{7,6},{8,9},{9,8},{10,11... | collective-permute-start | bytes 2654216 | tf_op jit(solution)/shard_map/ppermute | solution.py:198
  271.3 13.2 %copy-start.60 = (f32[768]{0:T(1024)S(1)}, f32[768]{0:T(1024)}, u32[]{:S(2)}) copy-start(f32[768]{0:T(1024)} %copy-done.59) | copy-start | bytes 9220
  271.3 13.2 %copy-start.63 = (f32[2,256]{1,0:T(2,128)S(1)}, f32[2,256]{1,0:T(2,128)}, u32[]{:S(2)}) copy-start(f32[2,256]{1,0:T(2,128)} %copy-done.62) | copy-start | bytes 6148
  271.3 13.2 %copy-start.83 = (f32[2,256]{1,0:T(2,128)S(1)}, f32[2,256]{1,0:T(2,128)}, u32[]{:S(2)}) copy-start(f32[2,256]{1,0:T(2,128)} %copy-done.82) | copy-start | bytes 6148
  275.2 9.3 %copy-start.3 = (f32[2,256,768]{2,1,0:T(8,128)S(1)}, f32[2,256,768]{2,1,0:T(8,128)}, u32[]{:S(2)}) copy-start(f32[2,256,768]{2,1,0:T(8,128)} %copy-done.2) | copy-start | bytes 4718596
  275.2 12.0 %copy-start.81 = (f32[2,256]{1,0:T(2,128)S(1)}, f32[2,256]{1,0:T(2,128)}, u32[]{:S(2)}) copy-start(f32[2,256]{1,0:T(2,128)} %copy-done.80) | copy-start | bytes 6148
  281.6 8.9 %copy-start.28 = (bf16[2,256,768]{2,1,0:T(8,128)(2,1)S(1)}, bf16[2,256,768]{2,1,0:T(8,128)(2,1)}, u32[]{:S(2)}) copy-start(bf16[2,256,768]{2,1,0:T(8,128)(2,1)} %param.26) | copy-start | bytes 2359300
  282.7 9.6 %copy-start.48 = (bf16[384,768]{1,0:T(8,128)(2,1)S(1)}, bf16[384,768]{1,0:T(8,128)(2,1)}, u32[]{:S(2)}) copy-start(bf16[384,768]{1,0:T(8,128)(2,1)} %param.20) | copy-start | bytes 1769476
  282.7 55.3 %collective-permute-start.17 = (bf16[768,512]{1,0:T(8,128)(2,1)}, bf16[768,512]{1,0:T(8,128)(2,1)}, u32[]{:S(2)}, u32[]{:S(2)}) collective-permute-start(bf16[768,512]{1,0:T(8,128)(2,1)} %bitcast.356), channel_id=1, source_target_pairs={{0,1},{1,0},{2,3},{3,2},{4,5},{5,4},{6,7},{7,6},{8,9},{9,8},{10,11... | collective-permute-start | bytes 2359304 | tf_op jit(solution)/shard_map/ppermute | solution.py:198
  328.1 7.3 %copy-start.38 = (bf16[2,6,64,256]{3,2,1,0:T(8,128)(2,1)S(1)}, bf16[2,6,64,256]{3,2,1,0:T(8,128)(2,1)}, u32[]{:S(2)}) copy-start(bf16[2,6,64,256]{3,2,1,0:T(8,128)(2,1)} %copy-done.37) | copy-start | bytes 1179652
  338.0 9.4 %copy-start.8 = (bf16[2,256,768]{2,1,0:T(8,128)(2,1)S(1)}, bf16[2,256,768]{2,1,0:T(8,128)(2,1)}, u32[]{:S(2)}) copy-start(bf16[2,256,768]{2,1,0:T(8,128)(2,1)} %param.14) | copy-start | bytes 2359300
  338.0 9.4 %copy-start.56 = (f32[768]{0:T(1024)S(1)}, f32[768]{0:T(1024)}, u32[]{:S(2)}) copy-start(f32[768]{0:T(1024)} %copy-done.55) | copy-start | bytes 9220
  338.0 9.4 %copy-start.58 = (f32[2,256]{1,0:T(2,128)S(1)}, f32[2,256]{1,0:T(2,128)}, u32[]{:S(2)}) copy-start(f32[2,256]{1,0:T(2,128)} %copy-done.57) | copy-start | bytes 6148
  338.0 9.4 %copy-start.75 = (f32[2,256]{1,0:T(2,128)S(1)}, f32[2,256]{1,0:T(2,128)}, u32[]{:S(2)}) copy-start(f32[2,256]{1,0:T(2,128)} %copy-done.74) | copy-start | bytes 6148
  347.2 156.6 %collective-permute-start.15 = (bf16[2,256,768]{2,1,0:T(8,128)(2,1)}, bf16[2,256,768]{2,1,0:T(8,128)(2,1)}, u32[]{:S(2)}, u32[]{:S(2)}) collective-permute-start(bf16[2,256,768]{2,1,0:T(8,128)(2,1)} %bitcast_convert_fusion.3), channel_id=1, source_target_pairs={{0,1},{1,0},{2,3},{3,2},{4,5},{5,4},{6,7},{7,6},{8,9},{9,8},{10,11... | collective-permute-start | bytes 2359304 | tf_op jit(solution)/shard_map/ppermute | solution.py:198
  484.4 7.5 %copy-start.32 = (bf16[768,1536]{1,0:T(8,128)(2,1)S(1)}, bf16[768,1536]{1,0:T(8,128)(2,1)}, u32[]{:S(2)}) copy-start(bf16[768,1536]{1,0:T(8,128)(2,1)} %get-tuple-element.21) | copy-start | bytes 7077892
  497.3 8.4 %copy-start.79 = (f32[2,256]{1,0:T(2,128)S(1)}, f32[2,256]{1,0:T(2,128)}, u32[]{:S(2)}) copy-start(f32[2,256]{1,0:T(2,128)} %copy-done.78) | copy-start | bytes 6148
  498.6 9.4 %copy-start.77 = (f32[2,256]{1,0:T(2,128)S(1)}, f32[2,256]{1,0:T(2,128)}, u32[]{:S(2)}) copy-start(f32[2,256]{1,0:T(2,128)} %copy-done.76) | copy-start | bytes 6148
  501.3 6.7 %copy-start.30 = (bf16[2,256,768]{2,1,0:T(8,128)(2,1)S(1)}, bf16[2,256,768]{2,1,0:T(8,128)(2,1)}, u32[]{:S(2)}) copy-start(bf16[2,256,768]{2,1,0:T(8,128)(2,1)} %param.26) | copy-start | bytes 2359300
  502.6 8.4 %copy-start.89 = (f32[1,768]{1,0:T(1,128)S(1)}, f32[1,768]{1,0:T(1,128)}, u32[]{:S(2)}) copy-start(f32[1,768]{1,0:T(1,128)} %stack.103) | copy-start | bytes 9220
  502.7 8.4 %copy-start.88 = (f32[1,768]{1,0:T(1,128)S(1)}, f32[1,768]{1,0:T(1,128)}, u32[]{:S(2)}) copy-start(f32[1,768]{1,0:T(1,128)} %stack.106) | copy-start | bytes 9220
  502.7 8.4 %copy-start.94 = (f32[1536]{0:T(1024)S(1)}, f32[1536]{0:T(1024)}, u32[]{:S(2)}) copy-start(f32[1536]{0:T(1024)} %get-tuple-element.162) | copy-start | bytes 18436
  (67 other events, 250.4 us)
Sparse Core Ops, SparseCore 0:
  17.2 12.4 all-gather.2
  323.0 9.0 reduce-scatter.1

commit v2 on v1

--- a/solution.py
+++ b/solution.py
@@ -192,6 +192,417 @@
             collective_id=0, has_side_effects=True, vmem_limit_bytes=60 * 2**20
         ),
     )(*arrays)
+
+
+DEPTH = 8
+SIDE = 8
+WIDE = 16
+CH = 128
+PAIR = 2 * CH
+ROWS = DEPTH * SIDE * WIDE
+TAPS = [(deep, wide) for deep in range(3) for wide in range(3)]
+PADDED_TAPS = 28
+
+
+def nt_dot(left, right):
+    return lax.dot_general(
+        left, right, (((1,), (1,)), ((), ())), preferred_element_type=jnp.float32
+    )
+
+
+def tn_dot(left, right):
+    return lax.dot_general(
+        left, right, (((0,), (0,)), ((), ())), preferred_element_type=jnp.float32
+    )
+
+
+def dot(left, right):
+    return jnp.dot(left, right, preferred_element_type=jnp.float32)
+
+
+def half_sums(row):
+    return row[:, :CH] + row[:, CH:]
+
+
+def twice(row):
+    return jnp.concatenate([row, row], axis=1)
+
+
+def row_and_column(size):
+    return (
+        lax.broadcasted_iota(jnp.int32, (size, size), 0),
+        lax.broadcasted_iota(jnp.int32, (size, size), 1),
+    )
+
+
+def shift_matrix(step):
+    row, column = row_and_column(PAIR)
+    same = (row // WIDE) == (column // WIDE)
+    return jnp.where(same & (row + step == column), 1.0, 0.0).astype(jnp.bfloat16)
+
+
+def weave_matrix():
+    row, column = row_and_column(PAIR)
+    source = lax.rem(row, 2) * CH + row // WIDE * SIDE + lax.rem(row, WIDE) // 2
+    return jnp.where(source == column, 1.0, 0.0).astype(jnp.bfloat16)
+
+
+def unweave_matrix():
+    row, column = row_and_column(PAIR)
+    source = lax.rem(column, 2) * CH + column // WIDE * SIDE + lax.rem(column, WIDE) // 2
+    return jnp.where(source == row, 1.0, 0.0).astype(jnp.bfloat16)
+
+
+def lay_kernel(kernels_ref, index, weights):
+    zero = jnp.zeros((CH, CH), jnp.bfloat16)
+    for at, (deep, wide) in enumerate(TAPS):
+        weights[at, 3 * CH :, :CH] = zero
+        weights[at, :CH, CH:] = zero
+        for high in range(3):
+            offset = ((deep * 3 + high) * 3 + wide) * CH
+            block = kernels_ref[index, offset : offset + CH, :]
+            weights[at, high * CH : (high + 1) * CH, :CH] = block
+            weights[at, (high + 1) * CH : (high + 2) * CH, CH:] = block
+
+
+def lay_flipped(kernels_ref, index, weights):
+    zero = jnp.zeros((CH, CH), jnp.bfloat16)
+    for at, (deep, wide) in enumerate(TAPS):
+        weights[at, :CH, 3 * CH :] = zero
+        weights[at, CH:, :CH] = zero
+        for high in range(3):
+            offset = (((2 - deep) * 3 + 2 - high) * 3 + 2 - wide) * CH
+            block = kernels_ref[index, offset : offset + CH, :]
+            weights[at, :CH, high * CH : (high + 1) * CH] = block
+            weights[at, CH:, (high + 1) * CH : (high + 2) * CH] = block
+
+
+def four_heights(field, wide, start, count):
+    depths = pl.ds(start, count)
+    low = field[wide, depths, 0:SIDE, :, CH:]
+    middle = field[wide, depths, 1 : SIDE + 1, :, :]
+    high = field[wide, depths, 2 : SIDE + 2, :, :CH]
+    joined = jnp.concatenate([low, middle, high], axis=-1)
+    return joined.reshape(count * SIDE * WIDE, 4 * CH)
+
+
+def conv_tile(field, weights, multiply, level, start):
+    total = None
+    for at, (deep, wide) in enumerate(TAPS):
+        product = multiply(four_heights(field, wide, start + deep, 2), weights[at])
+        total = product if total is None else total + product
+    level[pl.ds(pl.multiple_of(start * CH, 2 * CH), 2 * CH), :] = total
+
+
+def conv(field, weights, multiply, level, arrive):
+    @pl.loop(0, 2)
+    def _(step):
+        conv_tile(field, weights, multiply, level, 2 + 2 * step)
+
+    arrive()
+
+    @pl.loop(0, 2)
+    def _(step):
+        conv_tile(field, weights, multiply, level, 6 * step)
+
+
+def clear_rims(field, blk):
+    for wide in range(3):
+        field[wide, :, 0] = jnp.zeros((DEPTH + 2, WIDE, PAIR), jnp.bfloat16)
+        field[wide, :, SIDE + 1] = jnp.zeros((DEPTH + 2, WIDE, PAIR), jnp.bfloat16)
+        field[wide, 9 * blk] = jnp.zeros((SIDE + 2, WIDE, PAIR), jnp.bfloat16)
+
+
+def place_rows(field, before, after, step, value):
+    shape = (2, SIDE, WIDE, PAIR)
+    depths = pl.ds(1 + 2 * step, 2)
+    field[1, depths, 1 : SIDE + 1] = value.reshape(shape)
+    field[0, depths, 1 : SIDE + 1] = dot(before, value).astype(jnp.bfloat16).reshape(shape)
+    field[2, depths, 1 : SIDE + 1] = dot(after, value).astype(jnp.bfloat16).reshape(shape)
+
+
+def kernel_grad(field, dlevel_turned, index, out, tensor_half):
+    for at, (deep, wide) in enumerate(TAPS):
+        joined = four_heights(field, wide, deep, DEPTH)
+        block = dot(dlevel_turned[...], joined)
+        for high in range(3):
+            part = (
+                block[:CH, high * CH : (high + 1) * CH]
+                + block[CH:, (high + 1) * CH : (high + 2) * CH]
+            )
+            offset = ((deep * 3 + high) * 3 + wide) * CH
+            turned = part.T.astype(jnp.bfloat16)
+            for half in range(2):
+                out[half, offset : offset + CH, index * 64 : (index + 1) * 64] = turned[
+                    :, half * 64 : (half + 1) * 64
+                ]
+
+
+def decoder_kernel(
+    tapped,
+    tconv,
+    kernels,
+    grad_decoded,
+    mask,
+    inverse,
+    decoded,
+    block_all,
+    dtap_all,
+    grad_tconv,
+    grad_kernels,
+    field_one,
+    field_two,
+    dlevel_two,
+    dlevel_one,
+    weights_one,
+    weights_two,
+    flipped_two,
+    flipped_one,
+    level_one,
+    level_two,
+    dfield,
+    turned_two,
+    turned_one,
+    dlifted,
+    tapped_from,
+    dtap_mine,
+    dtap_from,
+    sums_mine,
+    sums_from,
+    send,
+    recv,
+):
+    dp, blk, tensor, near, far, first = place()
+    core, cross, beside, along = peers()
+    greet([core, cross])
+    low = jnp.bfloat16
+    row_tiles = ROWS // PAIR
+
+    copies = []
+
+    def start(index, src, dst, device):
+        copy = remote(src, dst, send.at[index], recv.at[index], device)
+        copy.start()
+        copies.append(copy)
+        return copy
+
+    give_tapped = start(0, tapped, tapped_from, cross)
+
+    before, after = shift_matrix(-1), shift_matrix(1)
+
+    def send_edge(index, field):
+        return start(
+            index,
+            field.at[:, DEPTH - 7 * blk, 1 : SIDE + 1],
+            field.at[:, 9 * blk, 1 : SIDE + 1],
+            core,
+        )
+
+    def rows_of(step):
+        return pl.ds(pl.multiple_of(step * PAIR, PAIR), PAIR)
+
+    def mask_rows(step):
+        return twice(mask[rows_of(step), :])
+
+    def totals(slot, pair):
+        sums_mine[slot, 0:1, :] = half_sums(pair[0])
+        sums_mine[slot, 1:2, :] = half_sums(pair[1])
+        return start(5 + slot, sums_mine.at[slot], sums_from.at[slot], core)
+
+    def means(slot, copy):
+        copy.wait_recv()
+        both = (sums_mine[slot] + sums_from[slot]) * inverse[...]
+        return both[0:1, :], both[1:2, :]
+
+    zero_pair = (jnp.zeros((1, PAIR), jnp.float32), jnp.zeros((1, PAIR), jnp.float32))
+
+    for field in (field_one, field_two, dlevel_two, dlevel_one):
+        clear_rims(field, blk)
+    weave = weave_matrix()
+    for piece in range(2):
+        tokens = slice(piece * CH, (piece + 1) * CH)
+        for a in range(2):
+            lifted = dot(tapped[tokens, :], tconv[:, a * 512 : (a + 1) * 512])
+            side = [
+                jnp.concatenate([lifted[:, c * CH : (c + 1) * CH],
+                                 lifted[:, (2 + c) * CH : (3 + c) * CH]], axis=1)
+                for c in range(2)
+            ]
+            woven = dot(weave, jnp.concatenate(side, axis=0).astype(low))
+            for depth in range(2):
+                at = 2 * (2 * piece + depth) + a
+                rows = slice(depth * CH, (depth + 1) * CH)
+                value = woven[rows, :] * twice(mask[at * CH : (at + 1) * CH, :])
+                level_one[at * CH : (at + 1) * CH, :] = value
+
+    @pl.loop(0, row_tiles)
+    def _(step):
+        place_rows(field_one, before, after, step, level_one[rows_of(step), :].astype(low))
+
+    edge = send_edge(1, field_one)
+    lay_kernel(kernels, 0, weights_one)
+    conv(field_one, weights_one, dot, level_one, edge.wait_recv)
+
+    def forward_sums(level):
+        def add(step, pair):
+            value = level[rows_of(step), :]
+            kept = value * mask_rows(step)
+            return (
+                pair[0] + jnp.sum(kept, axis=0, keepdims=True),
+                pair[1] + jnp.sum(kept * value, axis=0, keepdims=True),
+            )
+
+        return lax.fori_loop(0, row_tiles, add, zero_pair)
+
+    def mean_and_scale(slot, copy):
+        mean, second = means(slot, copy)
+        return twice(mean), twice(lax.rsqrt(second - mean * mean + 1e-05))
+
+    def sigmoid(value):
+        return 0.5 * jnp.tanh(0.5 * value) + 0.5
+
+    copy = totals(0, forward_sums(level_one))
+    lay_kernel(kernels, 1, weights_two)
+    mean_one, scale_one = mean_and_scale(0, copy)
+
+    @pl.loop(0, row_tiles)
+    def _(step):
+        normed = (level_one[rows_of(step), :] - mean_one) * scale_one
+        level_one[rows_of(step), :] = normed
+        value = normed * sigmoid(normed) * mask_rows(step)
+        place_rows(field_two, before, after, step, value.astype(low))
+
+    edge = send_edge(2, field_two)
+    lay_flipped(kernels, 1, flipped_two)
+    conv(field_two, weights_two, dot, level_two, edge.wait_recv)
+    copy = totals(1, forward_sums(level_two))
+    lay_flipped(kernels, 0, flipped_one)
+    mean_two, scale_two = mean_and_scale(1, copy)
+
+    def two_depths(ref, step, b):
+        return ref[pl.ds(2 * step, 2), :, b].reshape(PAIR, CH)
+
+    def decode(step, pair):
+        normed = (level_two[rows_of(step), :] - mean_two) * scale_two
+        level_two[rows_of(step), :] = normed
+        kept = mask_rows(step)
+        gate = sigmoid(normed)
+        value = (normed * gate * kept).astype(low)
+        for b in range(2):
+            decoded[pl.ds(2 * step, 2), :, b] = value[:, b * CH : (b + 1) * CH].reshape(
+                2, SIDE, WIDE, CH
+            )
+        grad = jnp.concatenate(
+            [two_depths(grad_decoded, step, 0), two_depths(grad_decoded, step, 1)], axis=1
+        ).astype(jnp.float32)
+        dnormed = gate * (1.0 + normed * (1.0 - gate)) * kept * grad
+        dfield[rows_of(step), :] = dnormed
+        return (
+            pair[0] + jnp.sum(dnormed, axis=0, keepdims=True),
+            pair[1] + jnp.sum(dnormed * normed, axis=0, keepdims=True),
+        )
+
+    copy = totals(2, lax.fori_loop(0, row_tiles, decode, zero_pair))
+
+    def level_grad(slot, copy, level, scale, field, turned):
+        mean_grad, mean_cross = means(slot, copy)
+        mean_grad, mean_cross = twice(mean_grad), twice(mean_cross)
+
+        @pl.loop(0, row_tiles)
+        def _(step):
+            centred = mean_grad + level[rows_of(step), :] * mean_cross
+            value = scale * (dfield[rows_of(step), :] - mask_rows(step) * centred)
+            place_rows(field, before, after, step, value.astype(low))
+            turned[:, rows_of(step)] = value.T.astype(low)
+
+    level_grad(2, copy, level_two, scale_two, dlevel_two, turned_two)
+    edge = send_edge(3, dlevel_two)
+    conv(dlevel_two, flipped_two, nt_dot, dfield, edge.wait_recv)
+
+    def back_one(step, pair):
+        normed = level_one[rows_of(step), :]
+        gate = sigmoid(normed)
+        dnormed = gate * (1.0 + normed * (1.0 - gate)) * mask_rows(step) * dfield[rows_of(step), :]
+        dfield[rows_of(step), :] = dnormed
+        return (
+            pair[0] + jnp.sum(dnormed, axis=0, keepdims=True),
+            pair[1] + jnp.sum(dnormed * normed, axis=0, keepdims=True),
+        )
+
+    copy = totals(3, lax.fori_loop(0, row_tiles, back_one, zero_pair))
+    level_grad(3, copy, level_one, scale_one, dlevel_one, turned_one)
+    edge = send_edge(4, dlevel_one)
+    conv(dlevel_one, flipped_one, nt_dot, dfield, edge.wait_recv)
+
+    unweave = unweave_matrix()
+    for piece in range(2):
+        tokens = slice(piece * CH, (piece + 1) * CH)
+        for a in range(2):
+            parts = []
+            for depth in range(2):
+                at = 2 * (2 * piece + depth) + a
+                rows = slice(at * CH, (at + 1) * CH)
+                parts.append(dfield[rows, :] * twice(mask[rows, :]))
+            apart = dot(unweave, jnp.concatenate(parts, axis=0).astype(low)).astype(low)
+            for c in range(2):
+                for b in range(2):
+                    column = ((a * 2 + b) * 2 + c) * CH
+                    dlifted[tokens, column : column + CH] = apart[
+                        c * CH : (c + 1) * CH, b * CH : (b + 1) * CH
+                    ]
+    dtap_mine[...] = nt_dot(dlifted[...], tconv[...]).astype(low)
+    give_dtap = start(9, dtap_mine, dtap_from, cross)
+    grad_tconv[...] = tn_dot(tapped[...], dlifted[...]).astype(low)
+    for half in range(2):
+        grad_kernels[half, 27 * CH :, :] = jnp.zeros((CH, CH), low)
+    kernel_grad(field_two, turned_two, 1, grad_kernels, tensor)
+    kernel_grad(field_one, turned_one, 0, grad_kernels, tensor)
+    give_tapped.wait_recv()
+    block_all[tensor] = tapped[...]
+    block_all[1 - tensor] = tapped_from[...]
+    give_dtap.wait_recv()
+    dtap_all[tensor] = dtap_mine[...]
+    dtap_all[1 - tensor] = dtap_from[...]
+    for copy in copies:
+        copy.wait_send()
+
+
+def decoder_section(tapped, tconv_weight, kernels, grad_decoded, mask, inverse):
+    low = jnp.bfloat16
+    vmem = pl.BlockSpec(memory_space=pltpu.VMEM)
+    field = pltpu.VMEM((3, DEPTH + 2, SIDE + 2, WIDE, PAIR), low)
+    plane = pltpu.VMEM((ROWS, PAIR), jnp.float32)
+    return pl.pallas_call(
+        decoder_kernel,
+        out_shape=[
+            jax.ShapeDtypeStruct((DEPTH, SIDE, 2, WIDE, CH), low),
+            jax.ShapeDtypeStruct((2,) + tapped.shape, low),
+            jax.ShapeDtypeStruct((2,) + tapped.shape, low),
+            jax.ShapeDtypeStruct(tconv_weight.shape, low),
+            jax.ShapeDtypeStruct((2, PADDED_TAPS * CH, CH), low),
+        ],
+        in_specs=[vmem] * 6,
+        out_specs=[vmem] * 5,
+        scratch_shapes=[field] * 4
+        + [pltpu.VMEM((9, 4 * CH, PAIR), low)] * 2
+        + [pltpu.VMEM((9, PAIR, 4 * CH), low)] * 2
+        + [plane] * 3
+        + [pltpu.VMEM((PAIR, ROWS), low)] * 2
+        + [
+            pltpu.VMEM((tapped.shape[0], tconv_weight.shape[1]), low),
+            pltpu.VMEM(tapped.shape, low),
+            pltpu.VMEM(tapped.shape, low),
+            pltpu.VMEM(tapped.shape, low),
+            pltpu.VMEM((4, 8, CH), jnp.float32),
+            pltpu.VMEM((4, 8, CH), jnp.float32),
+            pltpu.SemaphoreType.DMA((10,)),
+            pltpu.SemaphoreType.DMA((10,)),
+        ],
+        name="decoder_section",
+        compiler_params=pltpu.CompilerParams(
+            collective_id=1, has_side_effects=True, vmem_limit_bytes=60 * 2**20
+        ),
+    )(tapped, tconv_weight, kernels, grad_decoded, mask, inverse)
 
 
 def swap(value, axis):
@@ -409,59 +820,28 @@
         lax.dynamic_slice_in_dim(valid_full, first_item, per_device, 0), axis=1, keepdims=True
     )
     voxel_valid = voxel_mask(my_valid)
-    lifted = jnp.einsum("isd,dk->isk", tapped, tconv_weight, preferred_element_type=jnp.float32)
-    field_one = (to_voxels(lifted) * voxel_valid).astype(jnp.bfloat16)
-    padded_one, level = conv_forward(field_one, kernels[0])
-    normed_dec_one, scale_one = norm_forward(level, voxel_valid, voxel_count)
-    field_two = (jax.nn.silu(normed_dec_one) * voxel_valid).astype(jnp.bfloat16)
-    padded_two, level = conv_forward(field_two, kernels[1])
-    normed_dec_two, scale_two = norm_forward(level, voxel_valid, voxel_count)
-    decoded = (jax.nn.silu(normed_dec_two) * voxel_valid).astype(jnp.bfloat16)
-    channels = kernels.shape[2]
-    silu_two, silu_back_two = jax.vjp(jax.nn.silu, normed_dec_two)
-    dnormed = silu_back_two(grad_decoded.astype(jnp.float32) * voxel_valid)[0]
-    dlevel = norm_backward(dnormed, normed_dec_two, scale_two, voxel_valid, voxel_count).astype(
-        jnp.bfloat16
-    )
-    grad_kernel_two = jnp.einsum(
-        "rk,rc->kc",
-        columns_of(padded_two),
-        dlevel.reshape(-1, channels),
-        preferred_element_type=jnp.float32,
-    )
-    dfield_two = conv_input_grad(dlevel, kernels[1])
-    silu_one, silu_back_one = jax.vjp(jax.nn.silu, normed_dec_one)
-    dnormed = silu_back_one(dfield_two * voxel_valid)[0]
-    dlevel = norm_backward(dnormed, normed_dec_one, scale_one, voxel_valid, voxel_count).astype(
-        jnp.bfloat16
-    )
-    grad_kernel_one = jnp.einsum(
-        "rk,rc->kc",
-        columns_of(padded_one),
-        dlevel.reshape(-1, channels),
-        preferred_element_type=jnp.float32,
-    )
-    dfield_one = conv_input_grad(dlevel, kernels[0])
-    dlifted = from_voxels(dfield_one * voxel_valid).astype(jnp.bfloat16)
-    grad_tconv = jnp.einsum("isd,isk->dk", tapped, dlifted, preferred_element_type=jnp.float32)
-    dtapped = jnp.einsum("isk,dk->isd", dlifted, tconv_weight, preferred_element_type=jnp.float32)
-    grad_kernel_pair = jnp.stack([grad_kernel_one, grad_kernel_two])
+    mask = jnp.broadcast_to(
+        voxel_valid[0, :, ::2].reshape(ROWS, 1), (ROWS, CH)
+    )
+    inverse = jnp.broadcast_to(1.0 / voxel_count, (8, CH))
+    decoded, block_all, dtap_all, grad_tconv, kernel_halves = decoder_section(
+        tapped[0],
+        tconv_weight,
+        kernels,
+        grad_decoded.reshape(DEPTH, SIDE, 2, WIDE, CH),
+        mask,
+        inverse,
+    )
+    decoded = decoded.reshape(grad_decoded.shape)
     low = jnp.bfloat16
     mine = lax.axis_index("tensor")
     tconv_halves = grad_tconv.astype(low).reshape(768, 2, 512)
-    kernel_halves = (
-        grad_kernel_pair.astype(low).reshape(2, 3456, 2, 64).transpose(2, 1, 0, 3)
-        .reshape(2, 3456, 128)
-    )
     keep = lax.dynamic_index_in_dim(tconv_halves, mine, 1, False)
     give = lax.dynamic_index_in_dim(tconv_halves, 1 - mine, 1, False)
     tconv_part = (keep + swap(give, "tensor")).astype(low)
     keep = lax.dynamic_index_in_dim(kernel_halves, mine, 0, False)
     give = lax.dynamic_index_in_dim(kernel_halves, 1 - mine, 0, False)
-    kernel_part = jnp.pad((keep + swap(give, "tensor")).astype(low), ((0, 128), (0, 0)))
-    dtap_all = lax.all_gather(dtapped.astype(jnp.bfloat16), "tensor", axis=0, tiled=True).astype(
-        dtapped.dtype
-    )
+    kernel_part = (keep + swap(give, "tensor")).astype(low)
     dout = grad_out.astype(jnp.float32) + dtap_all
     ddown = dout.astype(jnp.bfloat16)
     grad_shift_three = jnp.sum(ddown.astype(jnp.float32), axis=(0, 1))

time: 593 us -> 456 us (0.77)
  local copies, waits for them, and re-layouts: 130 us -> 40 us
  Pallas kernels: 129 us -> 171 us
  matrix products: 84.6 us -> 46.8 us
  other arithmetic: 74.2 us -> 53.4 us
  starting transfers between devices: 28.4 us -> 8.51 us
  blocking collectives: 74.7 us -> 63.8 us
  waiting for transfers between devices: 43.4 us -> 51.2 us
    unnamed x367 -> x150, local copies, waits for them, and re-layouts: 55.3 us -> 8.31 us
    pallas_call x0 -> x1, Pallas kernels: none -> 42 us  [decoder_section(): pl.pallas_call(decoder_kernel, out_shape=[jax.ShapeDtypeStruct((DEPTH, SI...]
    dot_general x9 -> x0, matrix products: 36.4 us -> none  [the longest x2 12.2 us: conv_input_grad(): jnp.dot(columns_of(with_rims(dlevel)), flipped, preferred_element_type=jn...]
    ppermute x8 -> x0, starting transfers between devices: 20.1 us -> none  [the longest x4 15 us: extended(): lax.ppermute(lax.slice_in_dim(block, block.shape[dim] - width, None, axis...]
    all_gather x1 -> x0, blocking collectives: 10.5 us -> none  [body(): lax.all_gather(dtapped.astype(jnp.bfloat16), 'tensor', axis=0, tiled=True)]
    dot_general x3 -> x0, local copies, waits for them, and re-layouts: 9.54 us -> none  [the longest x1 3.64 us: body(): jnp.einsum('rk,rc->kc', columns_of(padded_two), dlevel.reshape(-1, channe...]
    ppermute x10 -> x6, waiting for transfers between devices: 32.3 us -> 41 us  [swap(): return lax.ppermute(value, axis, [(0, 1), (1, 0)])]
    concatenate x6 -> x0, local copies, waits for them, and re-layouts: 7.66 us -> none  [columns_of(): jnp.concatenate(pieces, axis=-1)]
  transfers between devices with their start and end apart: 20 -> 8, of which waited for: 3 -> 4; matrix products, arithmetic and copies ran while one was open for 23% -> 17% of each run, Pallas kernels for 22% -> 29%
where the time goes in v2:
time: 456 us; the launch traced here: 451 us
  Pallas kernels  171 us (38%)
  blocking collectives  63.8 us (14%)
  other arithmetic  53.4 us (12%)
  waiting for transfers between devices  51.2 us (11%)
  matrix products  46.8 us (10%)
  local copies, waits for them, and re-layouts  40 us (9%)
  between operations  16.3 us (4%)
  starting transfers between devices  8.51 us (2%)
    pallas_call x1, Pallas kernels, total_over_group(): pl.pallas_call(functools.partial(total_kernel, count), out_shape=[jax.Sha...  129 us
    psum x1, blocking collectives, body(): lax.psum((grad_gains, grad_shifts, grad_qv_bias, grad_up_bias), ('dp', 'b...  63.8 us
    pallas_call x1, Pallas kernels, decoder_section(): pl.pallas_call(decoder_kernel, out_shape=[jax.ShapeDtypeStruct((DEPTH, SI...  42 us
    ppermute x6, waiting for transfers between devices, swap(): return lax.ppermute(value, axis, [(0, 1), (1, 0)])  41 us
    all_gather x1, waiting for transfers between devices, body(): lax.all_gather(jnp.stack([keys, values]), 'blk', axis=2, tiled=True)  10.1 us
  transfers between devices with their start and end apart: 8, of which 4 were waited for; matrix products, arithmetic and copies ran while one was open for 17% of the time, Pallas kernels for 29%

profile of v2, /device:TPU:0, one launch (start us, length us, event | category | flops | bytes accessed | tf_op | source)
XLA Modules:
  0.0 451.3 jit_solution(13562922681932165873)
XLA Ops:
  7.3 1.5 convert_reduce_fusion.1
  8.8 1.5 fusion.38
  10.8 2.8 fusion.32
  13.8 1.0 fusion.83
  14.7 1.0 pad_maximum_fusion.3
  15.9 2.3 copy.61
  18.2 10.1 %all-gather.2.cloned.1.call-done = bf16[2,2,512,384]{3,2,0,1:T(8,128)(2,1)} async-done(((bf16[2,2,256,384]{3,2,0,1:T(8,128)(2,1)}), bf16[2,2,512,384]{3,2,0,1:T(8,128)(2,1)}) %all-gather.2.cloned.1.call-update) | async-done | bytes 1572880 | tf_op jit(solution)/shard_map/all_gather | solution.py:767
  28.4 2.7 fusion.84
  31.1 2.3 copy.62
  33.3 2.3 copy.60
  35.6 2.7 fusion.87
  38.4 2.0 fusion.3
  41.1 2.2 fusion.57
  43.9 1.8 collective-permute-start
  45.7 18.0 %collective-permute-done = bf16[2,256,768]{2,1,0:T(8,128)(2,1)S(1)} collective-permute-done((bf16[2,256,768]{2,1,0:T(8,128)(2,1)S(1)}, bf16[2,256,768]{2,1,0:T(8,128)(2,1)S(1)}, u32[]{:S(2)}, u32[]{:S(2)}) %collective-permute-start) | collective-permute-done | bytes 786464 | tf_op jit(solution)/shard_map/ppermute | solution.py:609
  65.9 1.5 convolution_add_fusion
  67.4 2.8 fusion.47
  70.3 1.7 collective-permute-start.1
  74.0 15.5 %collective-permute-done.1 = bf16[2,256,768]{2,1,0:T(8,128)(2,1)} collective-permute-done((bf16[2,256,768]{2,1,0:T(8,128)(2,1)}, bf16[2,256,768]{2,1,0:T(8,128)(2,1)}, u32[]{:S(2)}, u32[]{:S(2)}) %collective-permute-start.1) | collective-permute-done | bytes 786464 | tf_op jit(solution)/shard_map/ppermute | solution.py:609
  89.5 2.1 add_convert_fusion.1
  93.1 1.0 broadcast_in_dim.101.mask
  94.1 42.0 %decoder_section.1 = (bf16[8,8,2,16,128]{4,3,2,1,0:T(8,128)(2,1)}, bf16[2,256,768]{2,1,0:T(8,128)(2,1)}, bf16[2,256,768]{2,1,0:T(8,128)(2,1)}, bf16[768,1024]{1,0:T(8,128)(2,1)}, bf16[2,3584,128]{2,1,0:T(8,128)(2,1)}) custom-call(bf16[256,768]{1,0:T(8,128)(2,1)} %dynamic-slice_bitcast_fusion.1.tapped, bf16[768,1024]{1,0:T(8,128)(2,1)} %tconv.1, ...), custom_call_target="tpu_custom_call" | custom-call | tf_op jit(solution)/shard_map/decoder_section/pallas_call | solution.py:575
  136.2 5.6 %convert_reduce_fusion = (f32[1536]{0:T(1024)}, bf16[2,256,1536]{2,1,0:T(8,128)(2,1)S(1)}) fusion(f32[2,256,1536]{2,1,0:T(8,128)} %copy-done.71, bf16[1536,768]{1,0:T(8,128)(2,1)S(1)} %copy-done, bf16[2,256,768]{2,1,0:T(8,128)(2,1)} %get-tuple-element.24, bf16[2,256,768]{2,1,0:T(8,128)(2,1)S(1)} %copy-done.18), kind=kOutput, calls=%fused_computation.25 | convolution fusion | flops 1226832384 | bytes 8656896 | tf_op jit(solution)/shard_map/isd,fd->isf/dot_general | solution.py:849
  141.7 1.4 fusion.44
  143.1 1.4 collective-permute-start.2
  144.6 1.0 dynamic-slice_bitcast_fusion
  146.3 3.1 reshape.288
  149.3 4.4 constant_dynamic-slice_fusion.1
  153.7 1.1 copy.90
  154.8 1.4 collective-permute-start.5
  156.2 7.5 %collective-permute-done.2 = bf16[2,256,768]{2,1,0:T(8,128)(2,1)} collective-permute-done((bf16[2,256,768]{2,1,0:T(8,128)(2,1)S(1)}, bf16[2,256,768]{2,1,0:T(8,128)(2,1)}, u32[]{:S(2)}, u32[]{:S(2)}) %collective-permute-start.2) | collective-permute-done | bytes 786464 | tf_op jit(solution)/shard_map/ppermute | solution.py:609
  163.8 2.4 multiply_reduce_fusion
  166.3 2.0 fusion.81
  168.3 1.0 convert_reduce_fusion.3
  171.1 3.8 convolution_convert_fusion
  174.9 4.8 %fusion.50 = bf16[2,6,64,512]{3,2,1,0:T(8,128)(2,1)} fusion(bf16[2,256,6,64]{1,3,2,0:T(8,128)(2,1)S(1)} %bitcast.120, f32[2,6,256,512]{3,2,1,0:T(8,128)} %copy-done.2, f32[2,6,256]{2,1,0:T(8,128)S(1)} %log_add_fusion), kind=kOutput, calls=%fused_computation.77 | convolution fusion | flops 204865536 | bytes 7483392 | tf_op jit(solution)/shard_map/ihqk,iqhe->ikhe/dot_general | solution.py:887
  179.7 2.3 copy.69
  182.0 4.9 %fusion = f32[2,6,256]{2,1,0:T(8,128)S(1)} fusion(bf16[2,6,256,512]{3,2,1,0:T(8,128)(2,1)} %convolution_convert_fusion, f32[2,6,256,512]{3,2,1,0:T(8,128)} %copy-done.2, f32[2,6,256]{2,1,0:T(8,128)S(1)} %log_add_fusion), kind=kLoop, calls=%fused_computation.2 | loop fusion | flops 6288384 | bytes 9461760 | tf_op jit(solution)/shard_map/reduce_sum | solution.py:877
  186.9 3.9 fusion.2
  190.9 1.9 multiply_convert_fusion.1
  192.8 2.4 copy.68
  195.2 2.5 pad_maximum_fusion
  198.3 4.6 %bitcast_convert_fusion.refs_3_ = bf16[768,1536]{1,0:T(8,128)(2,1)} fusion(bf16[2,256,1536]{2,1,0:T(8,128)(2,1)} %copy-done.73, f32[2,256,768]{2,1,0:T(8,128)S(1)} %copy-done.4, f32[768]{0:T(1024)S(1)} %copy-done.65, f32[768]{0:T(1024)S(1)} %copy-done.45, f32[2,256]{1,0:T(2,128)S(1)} %copy-done.55, f32[2,256]{1,0:T(2,128)S(1)} %copy-done.47), kind=kOutput, calls=%fused_computation.11 | convolution fusion | flops 1211105280 | bytes 5515264 | tf_op jit(solution)/shard_map/isd,isf->df/dot_general | solution.py:853
  202.9 3.5 bitcast_convert_fusion.1.refs_2_
  206.5 1.2 convert_reduce_fusion.5
  210.8 2.3 fusion.60.refs_1_
  213.1 2.3 bitcast_add_fusion.refs_0_
  215.4 2.4 fusion.40
  217.9 2.2 copy.76
  220.1 3.8 bitcast_convert_fusion.3
  223.9 1.4 collective-permute-start.3
  225.4 129.4 %weight_sums.1 = (bf16[3584,128]{1,0:T(8,128)(2,1)}, bf16[768,512]{1,0:T(8,128)(2,1)}, bf16[1536,768]{1,0:T(8,128)(2,1)}, bf16[768,1536]{1,0:T(8,128)(2,1)}, bf1...) custom-call(bf16[3584,128]{1,0:T(8,128)(2,1)} %bitcast_add_fusion.refs_0_, bf16[768,512]{1,0:T(8,128)(2,1)} %fusion.60.refs_1_, ...), custom_call_target="tpu_custom_call" | custom-call | tf_op jit(solution)/shard_map/weight_sums/pallas_call | solution.py:183
  354.8 1.4 slice_convert_fusion
  356.4 1.4 convert_element_type.217
  358.0 2.0 convert.27
  360.0 2.2 copy.77
  362.2 4.6 %convert_element_type.214 = f32[768,1536]{1,0:T(8,128)} convert(bf16[768,1536]{1,0:T(8,128)(2,1)} %get-tuple-element.29) | non-fusion elementwise | flops 1179648 | bytes 7077888 | tf_op jit(solution)/shard_map/convert_element_type | solution.py:933
  366.8 2.5 convert_element_type.216
  369.5 1.1 pad_maximum_fusion.2
  370.6 2.0 fusion.39
  372.6 2.5 fusion.37
  375.2 3.1 convert_reduce_fusion.2
  378.3 63.8 %all-reduce = (f32[2,768]{1,0:T(2,128)}, f32[4,768]{1,0:T(4,128)}, f32[2,384]{1,0:T(2,128)}, f32[1536]{0:T(1024)}) all-reduce(f32[2,768]{1,0:T(2,128)S(1)} %pad_maximum_fusion.8, f32[4,768]{1,0:T(4,128)S(1)} %pad_maximum_fusion.7, f32[2,384]{1,0:T(2,128)S(1)} %pad_maximum_fusion.9, ...), channel_id=1, replica_groups=mesh['dp'=8,'blk'=2,'tensor'=2] {'dp','blk'}, use_global_device_ids=true, to_apply=%region_15.16 | all-reduce | flops 6912 | bytes 55296 | tf_op jit(solution)/shard_map/psum | solution.py:922
  442.1 1.9 copy.92
  (209 shorter events, 14.0 us)
Async XLA Ops:
  7.2 60.2 %copy-start = (bf16[1536,768]{1,0:T(8,128)(2,1)S(1)}, bf16[1536,768]{1,0:T(8,128)(2,1)}, u32[]{:S(2)}) copy-start(bf16[1536,768]{1,0:T(8,128)(2,1)} %param.23) | copy-start | bytes 7077892
  7.2 3.6 copy-start.8
  7.2 3.1 copy-start.66
  7.2 3.1 copy-start.59
  7.2 3.1 copy-start.61
  7.2 21.1 %all-gather.2.cloned.1.call-start = ((), (), s32[]{:S(2)}) async-start(), calls=%async_computation.1 | async-start | bytes 2359296 | tf_op jit(solution)/shard_map/all_gather | solution.py:767
  8.8 4.9 %copy-start.42 = (f32[2,256]{1,0:T(2,128)}, f32[2,256]{1,0:T(2,128)S(1)}, u32[]{:S(2)}) copy-start(f32[2,256]{1,0:T(2,128)S(1)} %broadcast_multiply_fusion.1) | copy-start | bytes 6148
  10.3 3.4 copy-start.48
  10.4 3.3 copy-start.40
  10.4 3.3 copy-start.62
  10.4 54.1 %copy-start.64 = (f32[768]{0:T(1024)}, f32[768]{0:T(1024)S(1)}, u32[]{:S(2)}) copy-start(f32[768]{0:T(1024)S(1)} %get-tuple-element.42) | copy-start | bytes 9220
  10.4 155.8 %copy-start.44 = (f32[768]{0:T(1024)}, f32[768]{0:T(1024)S(1)}, u32[]{:S(2)}) copy-start(f32[768]{0:T(1024)S(1)} %get-tuple-element.80) | copy-start | bytes 9220
  15.7 2.5 copy-start.70
  15.7 199.7 %reduce-scatter.2.cloned.1.call-start = ((), (), s32[]{:S(2)}) async-start(), calls=%async_computation.2 | async-start | bytes 2359296 | tf_op jit(solution)/shard_map/reduce_scatter | solution.py:899
  15.8 19.8 %copy-start.38 = (f32[6,64]{1,0:T(8,128)}, f32[6,64]{1,0:T(8,128)S(1)}, u32[]{:S(2)}) copy-start(f32[6,64]{1,0:T(8,128)S(1)} %add.208) | copy-start | bytes 4612
  38.3 2.7 copy-start.2
  38.4 2.7 copy-start.17
  41.1 2.2 copy-start.34
  43.2 20.9 %copy-start.31 = (bf16[2,6,64,256]{3,2,1,0:T(8,128)(2,1)}, bf16[2,6,64,256]{3,2,1,0:T(8,128)(2,1)S(1)}, u32[]{:S(2)}) copy-start(bf16[2,6,64,256]{3,2,1,0:T(8,128)(2,1)S(1)} %fusion.57) | copy-start | bytes 1179652
  43.9 19.8 %collective-permute-start = (bf16[2,256,768]{2,1,0:T(8,128)(2,1)S(1)}, bf16[2,256,768]{2,1,0:T(8,128)(2,1)S(1)}, u32[]{:S(2)}, u32[]{:S(2)}) collective-permute-start(bf16[2,256,768]{2,1,0:T(8,128)(2,1)S(1)} %convolution_convert_fusion.1), channel_id=1, source_target_pairs={{0,1},{1,0},{2,3},{3,2},{4,5},{5,4},{6,7},{7,6},{8,9},{9,8},{10,11... | collective-permute-start | bytes 2359304 | tf_op jit(solution)/shard_map/ppermute | solution.py:609
  63.7 2.2 copy-start.67
  64.1 1.8 copy-start.69
  64.1 102.1 %copy-start.46 = (f32[2,256]{1,0:T(2,128)}, f32[2,256]{1,0:T(2,128)S(1)}, u32[]{:S(2)}) copy-start(f32[2,256]{1,0:T(2,128)S(1)} %broadcast_multiply_fusion) | copy-start | bytes 6148
  64.5 101.8 %copy-start.54 = (f32[2,256]{1,0:T(2,128)}, f32[2,256]{1,0:T(2,128)S(1)}, u32[]{:S(2)}) copy-start(f32[2,256]{1,0:T(2,128)S(1)} %fusion.75) | copy-start | bytes 6148
  67.4 2.9 copy-start.71
  70.3 19.2 %collective-permute-start.1 = (bf16[2,256,768]{2,1,0:T(8,128)(2,1)}, bf16[2,256,768]{2,1,0:T(8,128)(2,1)}, u32[]{:S(2)}, u32[]{:S(2)}) collective-permute-start(bf16[2,256,768]{2,1,0:T(8,128)(2,1)} %fusion.47), channel_id=1, source_target_pairs={{0,1},{1,0},{2,3},{3,2},{4,5},{5,4},{6,7},{7,6},{8,9},{9,8},{10,11... | collective-permute-start | bytes 2359304 | tf_op jit(solution)/shard_map/ppermute | solution.py:609
  94.1 42.0 %copy-start.18 = (bf16[2,256,768]{2,1,0:T(8,128)(2,1)S(1)}, bf16[2,256,768]{2,1,0:T(8,128)(2,1)}, u32[]{:S(2)}) copy-start(bf16[2,256,768]{2,1,0:T(8,128)(2,1)} %param.26) | copy-start | bytes 2359300
  136.1 5.6 %copy-start.68 = (bf16[768,1536]{1,0:T(8,128)(2,1)S(1)}, bf16[768,1536]{1,0:T(8,128)(2,1)}, u32[]{:S(2)}) copy-start(bf16[768,1536]{1,0:T(8,128)(2,1)} %param.21) | copy-start | bytes 7077892
  141.7 2.9 copy-start.27
  143.1 20.6 %collective-permute-start.2 = (bf16[2,256,768]{2,1,0:T(8,128)(2,1)S(1)}, bf16[2,256,768]{2,1,0:T(8,128)(2,1)}, u32[]{:S(2)}, u32[]{:S(2)}) collective-permute-start(bf16[2,256,768]{2,1,0:T(8,128)(2,1)S(1)} %fusion.44), channel_id=1, source_target_pairs={{0,1},{1,0},{2,3},{3,2},{4,5},{5,4},{6,7},{7,6},{8,9},{9,8},{10,11... | collective-permute-start | bytes 2359304 | tf_op jit(solution)/shard_map/ppermute | solution.py:609
  145.6 67.5 %collective-permute-start.4 = (bf16[3584,128]{1,0:T(8,128)(2,1)}, bf16[3584,128]{1,0:T(8,128)(2,1)}, u32[]{:S(2)}, u32[]{:S(2)}) collective-permute-start(bf16[3584,128]{1,0:T(8,128)(2,1)} %dynamic-slice_bitcast_fusion), channel_id=1, source_target_pairs={{0,1},{1,0},{2,3},{3,2},{4,5},{5,4},{6,7},{7,6},{8,9},{9,8},{10,11... | collective-permute-start | bytes 2752520 | tf_op jit(solution)/shard_map/ppermute | solution.py:609
  153.7 10.0 %copy-start.4 = (f32[2,256,768]{2,1,0:T(8,128)S(1)}, f32[2,256,768]{2,1,0:T(8,128)}, u32[]{:S(2)}) copy-start(f32[2,256,768]{2,1,0:T(8,128)} %copy-done.3) | copy-start | bytes 4718596
  154.8 55.4 %collective-permute-start.5 = (bf16[768,512]{1,0:T(8,128)(2,1)}, bf16[768,512]{1,0:T(8,128)(2,1)}, u32[]{:S(2)}, u32[]{:S(2)}) collective-permute-start(bf16[768,512]{1,0:T(8,128)(2,1)} %bitcast.113), channel_id=1, source_target_pairs={{0,1},{1,0},{2,3},{3,2},{4,5},{5,4},{6,7},{7,6},{8,9},{9,8},{10,11... | collective-permute-start | bytes 2359304 | tf_op jit(solution)/shard_map/ppermute | solution.py:609
  166.3 2.0 copy-start.19
  166.3 2.0 copy-start.22
  168.3 2.0 copy-start.35
  182.0 4.9 %copy-start.7 = (bf16[2,6,256,512]{3,2,1,0:T(8,128)(2,1)S(1)}, bf16[2,6,256,512]{3,2,1,0:T(8,128)(2,1)}, u32[]{:S(2)}) copy-start(bf16[2,6,256,512]{3,2,1,0:T(8,128)(2,1)} %convolution_convert_fusion) | copy-start | bytes 9437188
  186.9 4.0 copy-start.11
  186.9 4.0 copy-start.39
  190.9 1.9 copy-start.5
  192.8 2.4 copy-start.16
  198.3 4.6 %copy-start.20 = (bf16[2,256,768]{2,1,0:T(8,128)(2,1)S(1)}, bf16[2,256,768]{2,1,0:T(8,128)(2,1)}, u32[]{:S(2)}) copy-start(bf16[2,256,768]{2,1,0:T(8,128)(2,1)} %param.26) | copy-start | bytes 2359300
  198.3 4.6 %copy-start.23 = (bf16[2,256,768]{2,1,0:T(8,128)(2,1)S(1)}, bf16[2,256,768]{2,1,0:T(8,128)(2,1)}, u32[]{:S(2)}) copy-start(bf16[2,256,768]{2,1,0:T(8,128)(2,1)} %get-tuple-element.24) | copy-start | bytes 2359300
  198.3 4.6 %copy-start.72 = (f32[2,256,1536]{2,1,0:T(8,128)S(1)}, f32[2,256,1536]{2,1,0:T(8,128)}, u32[]{:S(2)}) copy-start(f32[2,256,1536]{2,1,0:T(8,128)} %copy-done.71) | copy-start | bytes 9437188
  202.9 3.5 copy-start.6
  202.9 3.5 copy-start.12
  206.5 2.2 copy-start.15
  206.5 2.2 copy-start.32
  210.8 2.3 copy-start.28
  213.1 2.3 copy-start.36
  213.1 2.3 copy-start.41
  213.1 2.3 copy-start.43
  213.1 2.3 copy-start.49
  213.1 2.3 copy-start.63
  223.9 146.6 %collective-permute-start.3 = (bf16[2,256,768]{2,1,0:T(8,128)(2,1)}, bf16[2,256,768]{2,1,0:T(8,128)(2,1)}, u32[]{:S(2)}, u32[]{:S(2)}) collective-permute-start(bf16[2,256,768]{2,1,0:T(8,128)(2,1)} %bitcast_convert_fusion.3), channel_id=1, source_target_pairs={{0,1},{1,0},{2,3},{3,2},{4,5},{5,4},{6,7},{7,6},{8,9},{9,8},{10,11... | collective-permute-start | bytes 2359304 | tf_op jit(solution)/shard_map/ppermute | solution.py:609
  362.2 4.7 %copy-start.25 = (bf16[1536,768]{1,0:T(8,128)(2,1)S(1)}, bf16[1536,768]{1,0:T(8,128)(2,1)}, u32[]{:S(2)}) copy-start(bf16[1536,768]{1,0:T(8,128)(2,1)} %get-tuple-element.30) | copy-start | bytes 7077892
  366.8 2.6 copy-start.26
  370.6 2.0 copy-start.53
  370.6 4.5 %copy-start.24 = (bf16[2,256,768]{2,1,0:T(8,128)(2,1)S(1)}, bf16[2,256,768]{2,1,0:T(8,128)(2,1)}, u32[]{:S(2)}) copy-start(bf16[2,256,768]{2,1,0:T(8,128)(2,1)} %get-tuple-element.24) | copy-start | bytes 2359300
  372.6 2.6 copy-start.10
  372.6 2.6 copy-start.21
  372.6 2.6 copy-start.51
  375.1 3.2 copy-start.60
  375.1 68.8 %copy-start.1 = (bf16[1536,768]{1,0:T(8,128)(2,1)S(1)}, bf16[1536,768]{1,0:T(8,128)(2,1)}, u32[]{:S(2)}) copy-start(bf16[1536,768]{1,0:T(8,128)(2,1)} %param.23) | copy-start | bytes 7077892
  (18 other events, 20.6 us)
Sparse Core Ops, SparseCore 0:
  15.8 12.4 all-gather.1
  197.8 9.9 reduce-scatter.1
